TPU v7x, 512 devices: a whole 4x4x16 slice. The times are simulated.
512 devices in a mesh: group: 8 (over y, core), ctx: 64 (over x, z).
Axes of the slice: x: 4, y: 4, z: 16, core: 2. Of those that a mesh axis runs over, the one named last changes fastest.
Arguments:
- query: bfloat16 [8, 4096, 4096], P('group', 'ctx'), may hold values from -6 to 6
- keys: bfloat16 [8, 4096, 4096], P('group', 'ctx'), may hold values from -6 to 6
- values: bfloat16 [8, 4096, 4096], P('group', 'ctx'), may hold values from -6 to 6
- decay_exp: int32 [32], replicated, may hold values from 0 to 10
- gain: float32 [4096], replicated, may hold values from 0.1 to 1.9
- route: int32 [8, 64, 8], P(None, 'ctx'), may hold values from 0 to 63, as said below
Outputs:
- mixed: bfloat16 [8, 4096, 4096], P('group', 'ctx')
Inputs may be any that keep to these rules, and one draw needn't show every extreme that they name: For every context index c, route[:, c, :] names each place 0 to 63 exactly once.
All inputs are finite; a program needn't handle non-finite values.
Results may differ from a plain program's by a relative error of at most 0.0056.
Values may be sent and summed in bfloat16 or wider, within the bound.
No kernel may reach another device: no remote copies, remote signals or barrier semaphores. Data moves between devices by JAX's collectives and lax.ppermute only.
A program may use at most 64 MiB of HBM per device.

v0:
```python
import jax
import jax.numpy as jnp
from jax import lax
from jax.sharding import PartitionSpec as P


def prefix(value, axis, join, neutral):
    count, mine = (lax.axis_size(axis), lax.axis_index(axis))
    pieces = jax.tree.map(lambda part: lax.all_gather(part, axis), value)
    so_far = jax.tree.map(
        lambda part, zero: jnp.full_like(part, 0) + jnp.asarray(zero, part.dtype), value, neutral
    )

    def lap(position, so_far):
        longer = join(so_far, jax.tree.map(lambda part: part[position], pieces))
        return jax.tree.map(lambda new, old: jnp.where(position < mine, new, old), longer, so_far)

    return lax.fori_loop(0, count - 1, lap, so_far)


def scan_states(earlier, later):
    return (earlier[0] * later[0], later[0][:, None, None] * earlier[1] + later[1])


def carried(query_rows, prior_state, start_weight):
    product = jnp.einsum(
        "the,hef->thf",
        query_rows,
        prior_state.astype(jnp.bfloat16),
        preferred_element_type=jnp.float32,
    )
    return product * start_weight[:, :, None]


def on_device(query, keys, values, decay_exp, gain, route):
    groups = lax.axis_size("group")
    shards = lax.axis_size("ctx")
    tokens = query.shape[1]
    total_width = query.shape[2]
    head_count = decay_exp.shape[0]
    head_width = total_width // head_count
    local_heads = head_count // groups
    slice_width = local_heads * head_width
    block_rows = tokens * groups
    piece_rows = tokens // groups
    pieces_count = groups * groups
    seq_len = block_rows * shards
    group_index = lax.axis_index("group")
    local_exp = lax.dynamic_slice_in_dim(decay_exp, group_index * local_heads, local_heads)
    local_gain = lax.dynamic_slice_in_dim(gain, group_index * slice_width, slice_width)
    exponent = local_exp.astype(jnp.float32)
    decay_rates = jnp.exp2(exponent * exponent / 8.0) / (4.0 * seq_len)
    position = jnp.arange(block_rows, dtype=jnp.float32)
    end_weight = jnp.exp(-decay_rates[None, :] * (block_rows - 1 - position)[:, None])
    start_weight = jnp.exp(-decay_rates[None, :] * (position + 1.0)[:, None])
    block_decay = jnp.exp(-decay_rates * block_rows)
    piece_order = route[:, 0, :].reshape(pieces_count)
    places = lax.broadcasted_iota(jnp.int32, (pieces_count, pieces_count), 0)
    slots = lax.broadcasted_iota(jnp.int32, (pieces_count, pieces_count), 1)
    inverse = jnp.sum(jnp.where(piece_order[None, :] == places, slots, 0), axis=1)

    def depart(source):
        return source[0].reshape(tokens, groups, slice_width)

    def arrive(received):
        pieces = received.reshape(pieces_count, piece_rows, slice_width)
        return jnp.take(pieces, inverse, axis=0).reshape(block_rows, local_heads, head_width)

    sent_query, sent_keys, sent_values = (
        lax.all_to_all(depart(query), "group", split_axis=1, concat_axis=0, tiled=True),
        lax.all_to_all(depart(keys), "group", split_axis=1, concat_axis=0, tiled=True),
        lax.all_to_all(depart(values), "group", split_axis=1, concat_axis=0, tiled=True),
    )
    query_rows = arrive(sent_query)
    key_rows = arrive(sent_keys)
    value_rows = arrive(sent_values)
    weighted = (key_rows.astype(jnp.float32) * end_weight[:, :, None]).astype(jnp.bfloat16)
    block_state = jnp.einsum(
        "she,shf->hef", weighted, value_rows, preferred_element_type=jnp.float32
    )
    identity = (
        jnp.ones((local_heads,), jnp.float32),
        jnp.zeros((local_heads, head_width, head_width), jnp.float32),
    )
    prior_state = prefix((block_decay, block_state), "ctx", scan_states, identity)[1]
    from_prior = carried(query_rows, prior_state, start_weight)
    tile_rows = min(512, block_rows)
    scores = jnp.einsum("the,she->hts", query_rows, key_rows, preferred_element_type=jnp.float32)
    offset = (0 + jnp.arange(tile_rows, dtype=jnp.float32))[:, None] - jnp.arange(
        tile_rows, dtype=jnp.float32
    )[None, :]
    decay_grid = jnp.where(
        (offset >= 0)[None],
        jnp.exp(-decay_rates[:, None, None] * jnp.maximum(offset, 0.0)[None]),
        0.0,
    )
    weights = (scores * decay_grid).astype(jnp.bfloat16)
    tile_outputs = jnp.einsum(
        "hts,she->the", weights, value_rows, preferred_element_type=jnp.float32
    )
    combined = tile_outputs + from_prior
    inverse_rms = lax.rsqrt(jnp.mean(combined * combined, axis=-1, keepdims=True) + 1e-06)
    normalized = (combined * inverse_rms * local_gain.reshape(local_heads, head_width)).astype(
        jnp.bfloat16
    )
    normalized = normalized.reshape(pieces_count, piece_rows, slice_width)
    stored_order = jnp.take(normalized, piece_order, axis=0).reshape(block_rows, 1, slice_width)
    returned = lax.all_to_all(stored_order, "group", split_axis=0, concat_axis=1, tiled=True)
    return returned.reshape(1, tokens, total_width)


def solution(mesh):
    in_specs = (
        P("group", "ctx", None),
        P("group", "ctx", None),
        P("group", "ctx", None),
        P(),
        P(),
        P(None, "ctx", None),
    )
    out_specs = P("group", "ctx", None)
    return jax.shard_map(
        on_device, mesh=mesh, in_specs=in_specs, out_specs=out_specs, check_vma=False
    )
```

profile of v0, /device:TPU:1, one launch (start us, length us, event | category | flops | bytes accessed | tf_op | source)
XLA Modules:
  0.0 349.0 jit_solution(6359395743810643935)
XLA Ops:
  6.5 1.3 copy.60
  8.8 10.3 %all-to-all-start.1 = ((bf16[64,8,512]{2,0,1:T(8,128)(2,1)}), bf16[64,8,512]{2,0,1:T(8,128)(2,1)S(1)}, u32[]{:S(2)}, u32[]{:S(2)}) async-start(bf16[64,8,512]{2,0,1:T(8,128)(2,1)} %copy.44), calls=%async_computation.1 | async-start | bytes 1048576 | tf_op jit(solution)/shard_map/all_to_all | solution.py:70
  19.0 1.2 copy.61
  21.2 1.3 dynamic-slice
  23.2 5.3 %all-to-all-done.1 = bf16[64,8,512]{2,0,1:T(8,128)(2,1)S(1)} async-done(((bf16[64,8,512]{2,0,1:T(8,128)(2,1)}), bf16[64,8,512]{2,0,1:T(8,128)(2,1)S(1)}, u32[]{:S(2)}, u32[]{:S(2)}) %all-to-all-start.1) | async-done | bytes 524320 | tf_op jit(solution)/shard_map/all_to_all | solution.py:70
  28.5 4.3 %all-to-all-start.2 = ((bf16[64,8,512]{2,0,1:T(8,128)(2,1)}), bf16[64,8,512]{2,0,1:T(8,128)(2,1)S(1)}, u32[]{:S(2)}, u32[]{:S(2)}) async-start(bf16[64,8,512]{2,0,1:T(8,128)(2,1)} %copy.45), calls=%async_computation.2 | async-start | bytes 1048576 | tf_op jit(solution)/shard_map/all_to_all | solution.py:71
  36.4 5.9 %all-to-all-done.2 = bf16[64,8,512]{2,0,1:T(8,128)(2,1)S(1)} async-done(((bf16[64,8,512]{2,0,1:T(8,128)(2,1)}), bf16[64,8,512]{2,0,1:T(8,128)(2,1)S(1)}, u32[]{:S(2)}, u32[]{:S(2)}) %all-to-all-start.2) | async-done | bytes 524320 | tf_op jit(solution)/shard_map/all_to_all | solution.py:71
  42.3 4.3 %all-to-all-start = ((bf16[64,8,512]{2,0,1:T(8,128)(2,1)}), bf16[64,8,512]{2,0,1:T(8,128)(2,1)S(1)}, u32[]{:S(2)}, u32[]{:S(2)}) async-start(bf16[64,8,512]{2,0,1:T(8,128)(2,1)} %copy.43), calls=%async_computation | async-start | bytes 1048576 | tf_op jit(solution)/shard_map/all_to_all | solution.py:72
  47.8 8.3 %all-to-all-done = bf16[64,8,512]{2,0,1:T(8,128)(2,1)S(1)} async-done(((bf16[64,8,512]{2,0,1:T(8,128)(2,1)}), bf16[64,8,512]{2,0,1:T(8,128)(2,1)S(1)}, u32[]{:S(2)}, u32[]{:S(2)}) %all-to-all-start) | async-done | bytes 524320 | tf_op jit(solution)/shard_map/all_to_all | solution.py:72
  57.2 1.6 multiply_convert_fusion.2
  59.9 118.6 %all-reduce = f32[256]{0:T(256)S(1)} all-reduce(f32[256]{0:T(256)S(1)} %get-tuple-element.129), channel_id=2, replica_groups=mesh['group'=8,'ctx'=64] {'ctx'}, use_global_device_ids=true, to_apply=%add | all-reduce | flops 256 | bytes 2048
  179.9 3.7 %fusion.2 = f32[512,4,128]{0,2,1:T(8,128)} fusion(f32[512,512]{1,0:T(8,128)S(1)} %fusion.5, f32[4]{0:T(128)S(1)} %get-tuple-element.130, pred[512,512]{1,0:T(8,128)(4,1)} %fusion.6, bf16[512,4,128]{2,1,0:T(4,128)(2,1)S(1)} %reshape.138, bf16[512,4,128]{2,1,0:T(4,128)(2,1)S(1)} %reshape.134, bf16[512,4,128]{2,1,0:T(4,128)(2,1)S(1)} %reshape.136), kind=kOutput, calls=%fused_computation.9 | convolution fusion | flops 541065216 | bytes 3932176 | tf_op jit(solution)/shard_map/hts,she->the/dot_general | solution.py:98
  183.6 68.1 %all-gather.4.cloned.1.call-done = f32[256,128,128]{2,1,0:T(8,128)} async-done(((f32[4,128,128]{2,1,0:T(8,128)}), f32[256,128,128]{2,1,0:T(8,128)}) %all-gather.4.cloned.1.call-update) | async-done | bytes 16777232 | tf_op jit(solution)/shard_map/all_gather | solution.py:9
  251.7 69.1 %while.14 = (s32[]{:T(128)}, f32[4,128,128]{2,1,0:T(8,128)S(1)}, s32[]{:T(128)}, f32[64,4]{1,0:T(8,128)S(1)}, f32[64,4,128,128]{3,2,1,0:T(8,128)}, /*index=5*/s32[]{:T(128)}, s32[]{:T(128)}) while((s32[]{:T(128)}, f32[4,128,128]{2,1,0:T(8,128)S(1)}, s32[]{:T(128)}, f32[64,4]{1,0:T(8,128)S(1)}, f32[64,4,128,128]{3,2,1,0:T(8,128)}, ...), condition=%wide.region_2.4_spmd.clone, body=%wide.region_1.3_spmd.clone.sunk | while | flops 262148 | bytes 786593 | solution.py:18
  252.8 1.1 fusion.19
  253.9 1.1 fusion.19
  255.0 1.1 fusion.19
  256.1 1.1 fusion.19
  257.2 1.1 fusion.19
  258.3 1.1 fusion.19
  259.4 1.1 fusion.19
  260.5 1.1 fusion.19
  261.6 1.1 fusion.19
  262.7 1.1 fusion.19
  263.8 1.1 fusion.19
  264.9 1.1 fusion.19
  266.0 1.1 fusion.19
  267.1 1.1 fusion.19
  268.2 1.1 fusion.19
  269.3 1.1 fusion.19
  270.4 1.1 fusion.19
  271.5 1.1 fusion.19
  272.6 1.1 fusion.19
  273.7 1.1 fusion.19
  274.8 1.1 fusion.19
  275.9 1.1 fusion.19
  277.0 1.1 fusion.19
  278.0 1.1 fusion.19
  279.1 1.1 fusion.19
  280.2 1.1 fusion.19
  281.3 1.1 fusion.19
  282.4 1.1 fusion.19
  284.6 1.1 fusion.19
  285.7 1.1 fusion.19
  287.9 1.1 fusion.19
  290.1 1.1 fusion.19
  291.2 1.1 fusion.19
  293.4 1.1 fusion.19
  295.6 1.1 fusion.19
  297.8 1.1 fusion.19
  298.9 1.1 fusion.19
  301.1 1.1 fusion.19
  303.3 1.1 fusion.19
  305.5 1.1 fusion.19
  306.6 1.1 fusion.19
  308.8 1.1 fusion.19
  311.0 1.1 fusion.19
  312.1 1.1 fusion.19
  314.3 1.1 fusion.19
  316.5 1.1 fusion.19
  318.7 1.1 fusion.19
  319.7 1.1 fusion.19
  320.8 1.6 multiply_reduce_fusion
  325.8 14.4 %all_to_all.60 = bf16[8,2,16384]{2,1,0:T(2,128)(2,1)S(1)} all-to-all(bf16[8,2,16384]{2,1,0:T(2,128)(2,1)S(1)} %reshape.202), channel_id=1, replica_groups=mesh['group'=8,'ctx'=64] {'group'}, dimensions={0} | all-to-all | bytes 1048576 | tf_op jit(solution)/shard_map/all_to_all | solution.py:108
  (133 shorter events, 32.0 us)
Async XLA Ops:
  6.5 172.0 %copy-start = (f32[4096]{0:T(1024)S(1)}, f32[4096]{0:T(1024)}, u32[]{:S(2)}) copy-start(f32[4096]{0:T(1024)} %param.14) | copy-start | bytes 49156
  6.5 26.3 %copy-start.3 = (s32[32]{0:T(128)S(1)}, s32[32]{0:T(128)}, u32[]{:S(2)}) copy-start(s32[32]{0:T(128)} %param.13) | copy-start | bytes 388
  6.5 27.0 %copy-start.2 = (s32[8,1,8]{2,1,0:T(1,128)S(1)}, s32[8,1,8]{2,1,0:T(1,128)}, u32[]{:S(2)}) copy-start(s32[8,1,8]{2,1,0:T(1,128)} %param.15) | copy-start | bytes 772
  6.5 27.7 %copy-start.1 = (bf16[1,64,4096]{2,1,0:T(8,128)(2,1)S(1)}, bf16[1,64,4096]{2,1,0:T(8,128)(2,1)}, u32[]{:S(2)}) copy-start(bf16[1,64,4096]{2,1,0:T(8,128)(2,1)} %param.12) | copy-start | bytes 1572868
  8.8 19.8 %all-to-all-start.1 = ((bf16[64,8,512]{2,0,1:T(8,128)(2,1)}), bf16[64,8,512]{2,0,1:T(8,128)(2,1)S(1)}, u32[]{:S(2)}, u32[]{:S(2)}) async-start(bf16[64,8,512]{2,0,1:T(8,128)(2,1)} %copy.44), calls=%async_computation.1 | async-start | bytes 1048576 | tf_op jit(solution)/shard_map/all_to_all | solution.py:70
  28.5 13.8 %all-to-all-start.2 = ((bf16[64,8,512]{2,0,1:T(8,128)(2,1)}), bf16[64,8,512]{2,0,1:T(8,128)(2,1)S(1)}, u32[]{:S(2)}, u32[]{:S(2)}) async-start(bf16[64,8,512]{2,0,1:T(8,128)(2,1)} %copy.45), calls=%async_computation.2 | async-start | bytes 1048576 | tf_op jit(solution)/shard_map/all_to_all | solution.py:71
  42.3 13.8 %all-to-all-start = ((bf16[64,8,512]{2,0,1:T(8,128)(2,1)}), bf16[64,8,512]{2,0,1:T(8,128)(2,1)S(1)}, u32[]{:S(2)}, u32[]{:S(2)}) async-start(bf16[64,8,512]{2,0,1:T(8,128)(2,1)} %copy.43), calls=%async_computation | async-start | bytes 1048576 | tf_op jit(solution)/shard_map/all_to_all | solution.py:72
  46.6 205.1 %all-gather.4.cloned.1.call-start = ((), (), s32[]{:S(2)}) async-start(), calls=%async_computation.4 | async-start | bytes 17039360 | tf_op jit(solution)/shard_map/all_gather | solution.py:9
Sparse Core Ops, SparseCore 0:
  60.0 191.6 all-gather.3
where the time goes:
time: 352 us; the launch traced here: 349 us
  blocking collectives  133 us (38%)
  waiting for transfers between devices  87.5 us (25%)
  other arithmetic  71.7 us (20%)
  starting transfers between devices  18.8 us (5%)
  local copies, waits for them, and re-layouts  15.2 us (4%)
  between operations  14.3 us (4%)
  matrix products  6.38 us (2%)
    unnamed x1, blocking collectives  119 us
    all_gather x1, waiting for transfers between devices, prefix(): pieces = jax.tree.map(lambda part: lax.all_gather(part, axis), value)  68.1 us
    select_n x63, other arithmetic, lap(): jnp.where(position < mine, new, old)  66.3 us
    all_to_all x1, blocking collectives, on_device(): lax.all_to_all(stored_order, 'group', split_axis=0, concat_axis=1, tiled=...  14.4 us
    all_to_all x1, starting transfers between devices, on_device(): lax.all_to_all(depart(query), 'group', split_axis=1, concat_axis=0, tiled...  10.3 us
    all_to_all x1, waiting for transfers between devices, on_device(): lax.all_to_all(depart(values), 'group', split_axis=1, concat_axis=0, tile...  8.26 us
  transfers between devices with their start and end apart: 4, of which 4 were waited for; matrix products, arithmetic and copies ran while one was open for 4% of the time, Pallas kernels for 0%

commit v1 on v0

v1 whole, which is shorter than its diff:
```python
import functools

import jax
import jax.numpy as jnp
import numpy as np
from jax import lax
from jax.experimental import pallas as pl
from jax.experimental.pallas import tpu as pltpu
from jax.sharding import Mesh
from jax.sharding import PartitionSpec as P

BF = jnp.bfloat16
F32 = jnp.float32
Z = 16
E = 128
ROW = 8


def vmem():
    return pl.BlockSpec(memory_space=pltpu.VMEM)


def smem():
    return pl.BlockSpec(memory_space=pltpu.SMEM)


def params(**more):
    return pltpu.CompilerParams(vmem_limit_bytes=48 * 1024 * 1024, **more)


def decay_of(exp_ref, head):
    exponent = jnp.full((1, E), exp_ref[head], jnp.int32).astype(F32)
    return jnp.exp2(exponent * exponent / 8.0)


def pack(tokens, pieces, where_ref, route_ref, query, keys, values, out):
    heads = out.shape[0]
    first = where_ref[0] * pieces
    token = lax.broadcasted_iota(jnp.int32, (ROW, E), 1) % tokens
    places = jnp.zeros((ROW, E), jnp.int32)
    for piece in range(pieces):
        places = jnp.where(token // ROW == piece, route_ref[first + piece], places)
    places = places.astype(F32).astype(BF)
    for head in range(heads):
        columns = slice(head * E, (head + 1) * E)
        for at, source in enumerate((query, keys, values)):
            out[head, at * tokens : (at + 1) * tokens, :] = source[0, :, columns]
        out[head, 3 * tokens :, :] = places


def row_positions(received, tokens, block):
    lane = lax.broadcasted_iota(jnp.int32, (ROW, E), 1)
    step = (lane % ROW).astype(F32)
    chunks = []
    for pair in range(received.shape[0] // 2):
        even = received[2 * pair, block, 3 * tokens :, :].astype(F32)
        odd = received[2 * pair + 1, block, 3 * tokens :, :].astype(F32)
        chunks.append(jnp.where(lane < tokens, even, odd) * float(ROW) + step)
    return chunks


def column_positions(chunks):
    return jnp.concatenate(
        [jnp.transpose(jnp.broadcast_to(chunk[:1, :], (E, E))) for chunk in chunks], axis=0
    )


def states(tokens, scale, where_ref, exp_ref, received, out):
    groups, blocks = received.shape[:2]
    length = groups * tokens
    decay = decay_of(exp_ref, where_ref[1]) * scale
    found = []
    for block in range(blocks):
        position = column_positions(row_positions(received, tokens, block))
        weight = jnp.exp(-decay * (length - 1.0 - position))
        key_rows = received[:, block, tokens : 2 * tokens, :].reshape(length, E)
        value_rows = received[:, block, 2 * tokens : 3 * tokens, :].reshape(length, E)
        weighted = (key_rows.astype(F32) * weight).astype(BF)
        found.append(
            lax.dot_general(
                weighted, value_rows, (((0,), (0,)), ((), ())), preferred_element_type=F32
            )
        )
    for at in range(out.shape[0]):
        rows = slice(at * ROW, (at + 1) * ROW)
        out[at] = jnp.concatenate([state[rows] for state in found], axis=0).astype(BF)


def scan(length, scale, where_ref, exp_ref, pieces, out):
    steps, rows = pieces.shape[:2]
    decay = jnp.exp(-decay_of(exp_ref, where_ref[1]) * scale * length)
    total = jnp.zeros((ROW, E), F32)
    priors = [[None] * (rows // ROW) for _ in range(steps)]
    loaded = [pieces[step].astype(F32) for step in range(steps)]
    for block in range(rows // ROW):
        for step in range(steps):
            priors[step][block] = total
            total = total * decay + loaded[step][block * ROW : (block + 1) * ROW]
    for step in range(steps):
        out[step] = jnp.concatenate(priors[step], axis=0).astype(BF)


def attend(tokens, scale, where_ref, exp_ref, gain, received, prior, out):
    groups, blocks = received.shape[:2]
    length = groups * tokens
    middle = length / 2.0
    head = where_ref[1]
    decay = decay_of(exp_ref, head) * scale
    scaling = gain[pl.ds(head, 1), :]
    prior_weight = jnp.exp(-decay * (middle + 1.0))
    for block in range(blocks):
        chunks = row_positions(received, tokens, block)
        row = jnp.concatenate([chunk[:1] for chunk in chunks], axis=1)
        key_weight = jnp.exp(jnp.concatenate([decay] * len(chunks), axis=1) * (row - middle))
        column = column_positions(chunks)
        query_weight = jnp.exp(-decay * (column - middle))
        query_rows = received[:, block, :tokens, :].reshape(length, E)
        key_rows = received[:, block, tokens : 2 * tokens, :].reshape(length, E)
        value_rows = received[:, block, 2 * tokens : 3 * tokens, :].reshape(length, E)
        rows = slice(block * ROW, (block + 1) * ROW)
        state = jnp.concatenate(
            [prior[at].astype(F32)[rows] for at in range(prior.shape[0])], axis=0
        ).astype(BF)
        scores = lax.dot_general(
            query_rows, key_rows, (((1,), (1,)), ((), ())), preferred_element_type=F32
        )
        weights = jnp.where(column[:, :1] >= row, scores * key_weight, 0.0).astype(BF)
        combined = jnp.dot(weights, value_rows, preferred_element_type=F32)
        combined += jnp.dot(query_rows, state, preferred_element_type=F32) * prior_weight
        combined *= query_weight
        square = jnp.mean(combined * combined, axis=-1, keepdims=True)
        normal = (combined * lax.rsqrt(square + 1e-06) * scaling).astype(BF)
        out[:, block] = normal.reshape(groups, tokens, E)


def unpack(received, out):
    for head in range(received.shape[0]):
        out[0, :, head * E : (head + 1) * E] = received[head]


def on_device(query, keys, values, decay_exp, gain, route):
    groups = lax.axis_size("group")
    rows = lax.axis_size("x")
    tokens, width = query.shape[1:]
    heads = decay_exp.shape[0]
    pieces = tokens // ROW
    length = tokens * groups
    scale = 1.0 / (4.0 * length * rows * Z)
    group = lax.axis_index("group")
    where = jnp.stack([group, group * rows + lax.axis_index("x")]).astype(jnp.int32)
    sent_rows = 3 * tokens + ROW
    steps = 4
    sent = pl.pallas_call(
        functools.partial(pack, tokens, pieces),
        grid=(steps,),
        in_specs=[smem(), smem()]
        + [pl.BlockSpec((1, tokens, width // steps), lambda i: (0, 0, i))] * 3,
        out_specs=pl.BlockSpec((heads // steps, sent_rows, E), lambda i: (i, 0, 0)),
        out_shape=jax.ShapeDtypeStruct((heads, sent_rows, E), BF),
        compiler_params=params(),
        name="pack",
    )(where, route.reshape(groups * pieces), query, keys, values)
    received = lax.all_to_all(sent, ("group", "x"), split_axis=0, concat_axis=0, tiled=True)
    received = received.reshape(groups, rows, sent_rows, E)
    sliced = pl.pallas_call(
        functools.partial(states, tokens, scale),
        in_specs=[smem(), smem(), vmem()],
        out_specs=vmem(),
        out_shape=jax.ShapeDtypeStruct((Z, rows * ROW, E), BF),
        compiler_params=params(),
        name="states",
    )(where, decay_exp, received)
    sliced = lax.all_to_all(sliced, "z", split_axis=0, concat_axis=0, tiled=True)
    priors = pl.pallas_call(
        functools.partial(scan, length, scale),
        in_specs=[smem(), smem(), vmem()],
        out_specs=vmem(),
        out_shape=jax.ShapeDtypeStruct((Z, rows * ROW, E), BF),
        compiler_params=params(),
        name="scan",
    )(where, decay_exp, sliced)
    priors = lax.all_to_all(priors, "z", split_axis=0, concat_axis=0, tiled=True)
    mixed = pl.pallas_call(
        functools.partial(attend, tokens, scale),
        in_specs=[smem(), smem(), vmem(), vmem(), vmem()],
        out_specs=vmem(),
        out_shape=jax.ShapeDtypeStruct((groups, rows, tokens, E), BF),
        compiler_params=params(),
        name="attend",
    )(where, decay_exp, gain.reshape(heads, E), received, priors)
    mixed = mixed.reshape(heads, tokens, E)
    mixed = lax.all_to_all(mixed, ("group", "x"), split_axis=0, concat_axis=0, tiled=True)
    return pl.pallas_call(
        unpack,
        grid=(steps,),
        in_specs=[pl.BlockSpec((heads // steps, tokens, E), lambda i: (i, 0, 0))],
        out_specs=pl.BlockSpec((1, tokens, width // steps), lambda i: (0, 0, i)),
        out_shape=jax.ShapeDtypeStruct((1, tokens, width), BF),
        compiler_params=params(),
        name="unpack",
    )(mixed)


def solution(mesh):
    devices = np.asarray(mesh.devices)
    split = Mesh(devices.reshape(devices.shape[0], -1, Z), ("group", "x", "z"))
    ctx = ("x", "z")
    stored = P("group", ctx, None)
    in_specs = (stored, stored, stored, P(), P(), P(None, ctx, None))
    return jax.shard_map(
        on_device, mesh=split, in_specs=in_specs, out_specs=stored, check_vma=False
    )
```

time: 352 us -> 108 us (0.31)
  waiting for transfers between devices: 87.5 us -> 0 us
  other arithmetic: 71.7 us -> 1.41 us
  blocking collectives: 133 us -> 95 us
  starting transfers between devices: 18.8 us -> 0 us
  between operations: 14.3 us -> 0.04 us
  local copies, waits for them, and re-layouts: 15.2 us -> 3.79 us
  Pallas kernels: 0 us -> 6.98 us
  matrix products: 6.38 us -> 0 us
    unnamed x1 -> x0, blocking collectives: 119 us -> none
    all_to_all x1 -> x4, blocking collectives: 14.4 us -> 95 us  [the longest x1 32.8 us: on_device(): lax.all_to_all(sent, ('group', 'x'), split_axis=0, concat_axis=0, tiled=T...]
    all_gather x1 -> x0, waiting for transfers between devices: 68.1 us -> none  [prefix(): pieces = jax.tree.map(lambda part: lax.all_gather(part, axis), value)]
    select_n x66 -> x0, other arithmetic: 66.5 us -> none  [the longest x63 66.3 us: lap(): jnp.where(position < mine, new, old)]
    all_to_all x3 -> x0, waiting for transfers between devices: 19.4 us -> none  [the longest x1 8.26 us: on_device(): lax.all_to_all(depart(values), 'group', split_axis=1, concat_axis=0, tile...]
    all_to_all x3 -> x0, starting transfers between devices: 18.8 us -> none  [the longest x1 10.3 us: on_device(): lax.all_to_all(depart(query), 'group', split_axis=1, concat_axis=0, tiled...]
    pallas_call x0 -> x5, Pallas kernels: none -> 6.98 us  [the longest x1 2.57 us: on_device(): pl.pallas_call(functools.partial(attend, tokens, scale), in_specs=[smem()...]
    dot_general x3 -> x0, matrix products: 6.38 us -> none  [the longest x1 3.72 us: on_device(): jnp.einsum('hts,she->the', weights, value_rows, preferred_element_type=jn...]
  transfers between devices with their start and end apart: 4 -> 0, of which waited for: 4 -> 0; matrix products, arithmetic and copies ran while one was open for 4% -> 0% of each run, Pallas kernels for 0% -> 0%
where the time goes in v1:
time: 108 us; the launch traced here: 107 us
  blocking collectives  95 us (88%)
  Pallas kernels  6.98 us (6%)
  local copies, waits for them, and re-layouts  3.79 us (4%)
  other arithmetic  1.41 us (1%)
    all_to_all x1, blocking collectives, on_device(): lax.all_to_all(sent, ('group', 'x'), split_axis=0, concat_axis=0, tiled=T...  32.8 us
    all_to_all x1, blocking collectives, on_device(): lax.all_to_all(sliced, 'z', split_axis=0, concat_axis=0, tiled=True)  25.5 us
    all_to_all x1, blocking collectives, on_device(): lax.all_to_all(mixed, ('group', 'x'), split_axis=0, concat_axis=0, tiled=...  19 us
    all_to_all x1, blocking collectives, on_device(): lax.all_to_all(priors, 'z', split_axis=0, concat_axis=0, tiled=True)  17.7 us
    unnamed x11, local copies, waits for them, and re-layouts  3.71 us
    pallas_call x1, Pallas kernels, on_device(): pl.pallas_call(functools.partial(attend, tokens, scale), in_specs=[smem()...  2.57 us

profile of v1, /device:TPU:1, one launch (start us, length us, event | category | flops | bytes accessed | tf_op | source)
XLA Modules:
  0.0 107.2 jit_solution(18401897448439835316)
XLA Ops:
  0.0 0.6 broadcast.3
  0.6 1.3 %reduce.3 = s32[8,8]{1,0:T(8,128)S(1)} reduce(s32[8,1,8]{2,1,0:T(1,128)} %param.11, s32[]{:T(128)} %broadcast.3), dimensions={1}, to_apply=%param.11.reduce_sub_computation.3 | reduce | bytes 516 | tf_op args[5]
  1.9 0.1 reshape.13.route_ref
  2.0 0.1 pad_add_fusion.where_ref
  2.1 0.0 copy-start
  2.1 1.0 copy-done
  3.1 0.0 copy-start.1
  3.1 1.0 copy-done.1
  4.2 0.0 copy-start.2
  4.2 1.0 copy-done.2
  5.2 1.0 pack.1
  6.2 0.0 copy-start.4
  6.3 32.8 %all_to_all.20 = bf16[32,200,128]{2,1,0:T(8,128)(2,1)S(1)} all-to-all(bf16[32,200,128]{2,1,0:T(8,128)(2,1)S(1)} %pack.1), channel_id=1, replica_groups=mesh['group'=8,'x'=4,'z'=16] {'group','x'}, dimensions={0} | all-to-all | bytes 3276800 | tf_op jit(solution)/shard_map/all_to_all | solution.py:163
  39.1 0.0 copy-start.3
  39.1 0.0 copy-done.4
  39.1 1.3 %states.1 = bf16[16,32,128]{2,1,0:T(8,128)(2,1)S(1)} custom-call(s32[2]{0:T(128)S(1)} %pad_add_fusion.where_ref, s32[32]{0:T(128)S(1)} %copy-done.4, bf16[8,4,200,128]{3,2,1,0:T(8,128)(2,1)S(1)} %bitcast.5), custom_call_target="tpu_custom_call" | custom-call | tf_op jit(solution)/shard_map/states/pallas_call | solution.py:165
  40.4 25.5 %all_to_all.21.pieces = bf16[16,32,128]{2,1,0:T(8,128)(2,1)S(1)} all-to-all(bf16[16,32,128]{2,1,0:T(8,128)(2,1)S(1)} %states.1), channel_id=1, replica_groups=mesh['group'=8,'x'=4,'z'=16] {'z'}, dimensions={0} | all-to-all | bytes 262144 | tf_op jit(solution)/shard_map/all_to_all | solution.py:173
  65.8 0.7 scan.1
  66.5 17.7 %all_to_all.22.prior = bf16[16,32,128]{2,1,0:T(8,128)(2,1)S(1)} all-to-all(bf16[16,32,128]{2,1,0:T(8,128)(2,1)S(1)} %scan.1), channel_id=1, replica_groups=mesh['group'=8,'x'=4,'z'=16] {'z'}, dimensions={0} | all-to-all | bytes 262144 | tf_op jit(solution)/shard_map/all_to_all | solution.py:182
  84.2 0.0 copy-done.3
  84.2 2.6 %attend.1 = bf16[8,4,64,128]{3,2,1,0:T(8,128)(2,1)S(1)} custom-call(s32[2]{0:T(128)S(1)} %pad_add_fusion.where_ref, s32[32]{0:T(128)S(1)} %copy-done.4, f32[32,128]{1,0:T(8,128)S(1)} %bitcast.8, bf16[8,4,200,128]{3,2,1,0:T(8,128)(2,1)S(1)} %bitcast.6, bf16[16,32,128]{2,1,0:T(8,128)(2,1)S(1)} %all_to_all.22.prior), custom_call_target="tpu_custom_call" | custom-call | tf_op jit(solution)/shard_map/attend/pallas_call | solution.py:183
  86.8 19.0 %all_to_all.23.received = bf16[32,64,128]{2,1,0:T(8,128)(2,1)S(1)} all-to-all(bf16[32,64,128]{2,1,0:T(8,128)(2,1)S(1)} %bitcast.7), channel_id=1, replica_groups=mesh['group'=8,'x'=4,'z'=16] {'group','x'}, dimensions={0} | all-to-all | bytes 1048576 | tf_op jit(solution)/shard_map/all_to_all | solution.py:192
  105.8 1.4 %unpack.1 = bf16[1,64,4096]{2,1,0:T(8,128)(2,1)} custom-call(bf16[32,64,128]{2,1,0:T(8,128)(2,1)S(1)} %all_to_all.23.received), custom_call_target="tpu_custom_call" | custom-call | tf_op jit(solution)/shard_map/unpack/pallas_call | solution.py:193
Async XLA Ops:
  2.1 1.0 copy-start
  3.1 1.0 copy-start.1
  4.2 1.0 copy-start.2
  6.2 32.8 %copy-start.4 = (s32[32]{0:T(128)S(1)}, s32[32]{0:T(128)}, u32[]{:S(2)}) copy-start(s32[32]{0:T(128)} %exp_ref.5) | copy-start | bytes 388
  39.1 45.1 %copy-start.3 = (f32[4096]{0:T(1024)S(1)}, f32[4096]{0:T(1024)}, u32[]{:S(2)}) copy-start(f32[4096]{0:T(1024)} %param.10) | copy-start | bytes 49156

commit v2 on v1

v2 whole, which is shorter than its diff:
```python
import functools

import jax
import jax.numpy as jnp
import numpy as np
from jax import lax
from jax.experimental import pallas as pl
from jax.experimental.pallas import tpu as pltpu
from jax.sharding import Mesh
from jax.sharding import PartitionSpec as P

BF = jnp.bfloat16
F32 = jnp.float32
Z = 16
E = 128
ROW = 8


def vmem():
    return pl.BlockSpec(memory_space=pltpu.VMEM)


def smem():
    return pl.BlockSpec(memory_space=pltpu.SMEM)


def params(mebibytes=48):
    return pltpu.CompilerParams(vmem_limit_bytes=mebibytes * 1024 * 1024)


def my_head():
    return lax.axis_index("group") * lax.axis_size("x") + lax.axis_index("x")


def anywhere():
    return pl.BlockSpec(memory_space=pl.ANY)


def pack(tokens, pieces, route, query, keys, values, out, staged, route_ref, in_sems, out_sems, sem):
    heads = out.shape[0]
    parts = in_sems.shape[0]
    fetch = pltpu.make_async_copy(route, route_ref, sem)
    fetch.start()
    span = heads // parts
    for part in range(parts):
        for head in range(part * span, (part + 1) * span):
            for at, source in enumerate((query, keys, values)):
                pltpu.make_async_copy(
                    source.at[0, :, pl.ds(head * E, E)],
                    staged.at[head, pl.ds(at * tokens, tokens), :],
                    in_sems.at[part],
                ).start()
    token = lax.broadcasted_iota(jnp.int32, (ROW, E), 1) % tokens
    places = jnp.zeros((ROW, E), jnp.int32)
    group = lax.axis_index("group")
    fetch.wait()
    for piece in range(pieces):
        places = jnp.where(token // ROW == piece, route_ref[group, 0, piece], places)
    places = places.astype(F32).astype(BF)
    for head in range(heads):
        staged[head, 3 * tokens :, :] = places
    copies = []
    for part in range(parts):
        some = pl.ds(part * span, span)
        landed = staged.at[some, pl.ds(0, 3 * tokens), :]
        pltpu.make_async_copy(landed, landed, in_sems.at[part]).wait()
        copies.append(pltpu.make_async_copy(staged.at[some], out.at[some], out_sems.at[part]))
        copies[-1].start()
    for copy in copies:
        copy.wait()


def row_positions(received, tokens, block):
    lane = lax.broadcasted_iota(jnp.int32, (ROW, E), 1)
    step = (lane % ROW).astype(F32)
    chunks = []
    for pair in range(received.shape[0] // 2):
        even = received[2 * pair, block, 3 * tokens :, :].astype(F32)
        odd = received[2 * pair + 1, block, 3 * tokens :, :].astype(F32)
        chunks.append(jnp.where(lane < tokens, even, odd) * float(ROW) + step)
    return chunks


def column_positions(chunks):
    return jnp.concatenate(
        [jnp.transpose(jnp.broadcast_to(chunk[:1, :], (E, E))) for chunk in chunks], axis=0
    )


def states(tokens, scale, exp_ref, gain, received, out, constants):
    groups, blocks = received.shape[:2]
    length = groups * tokens
    head = my_head()
    exponent = jnp.full((ROW, E), exp_ref[head], jnp.int32).astype(F32)
    decay = jnp.exp2(exponent * exponent / 8.0) * scale
    constants[0] = decay
    constants[1] = jnp.broadcast_to(gain[pl.ds(head, 1), :], (ROW, E))
    wide = jnp.concatenate([decay[:1]] * (length // E), axis=1)
    found = []
    for block in range(blocks):
        chunks = row_positions(received, tokens, block)
        position = jnp.concatenate([chunk[:1] for chunk in chunks], axis=1)
        weight = jnp.exp(-wide * (length - 1.0 - position))
        key_rows = received[:, block, tokens : 2 * tokens, :].reshape(length, E)
        value_rows = received[:, block, 2 * tokens : 3 * tokens, :].reshape(length, E)
        weighted = (jnp.transpose(key_rows).astype(F32) * weight).astype(BF)
        found.append(jnp.dot(weighted, value_rows, preferred_element_type=F32))
    for at in range(out.shape[0]):
        rows = slice(at * ROW, (at + 1) * ROW)
        out[at] = jnp.concatenate([state[rows] for state in found], axis=0).astype(BF)


def scan(length, constants, pieces, out):
    steps, rows = pieces.shape[:2]
    decay = jnp.exp(-constants[0] * length)
    total = jnp.zeros((ROW, E), F32)
    priors = [[None] * (rows // ROW) for _ in range(steps)]
    loaded = [pieces[step].astype(F32) for step in range(steps)]
    for block in range(rows // ROW):
        for step in range(steps):
            priors[step][block] = total
            total = total * decay + loaded[step][block * ROW : (block + 1) * ROW]
    for step in range(steps):
        out[step] = jnp.concatenate(priors[step], axis=0).astype(BF)


def within(tokens, constants, received, out, query_weight):
    groups, blocks = received.shape[:2]
    length = groups * tokens
    middle = length / 2.0
    decay = constants[0][:1]
    prior_weight = jnp.exp(-decay * (middle + 1.0))
    lane = lax.broadcasted_iota(jnp.int32, (length, E), 1)
    query_weights = jnp.zeros((length, E), F32)
    for block in range(blocks):
        chunks = row_positions(received, tokens, block)
        row = jnp.concatenate([chunk[:1] for chunk in chunks], axis=1)
        key_weight = jnp.exp(jnp.concatenate([decay] * len(chunks), axis=1) * (row - middle))
        column = column_positions(chunks)
        weight = jnp.exp(-decay * (column - middle))
        query_rows = received[:, block, :tokens, :].reshape(length, E)
        key_rows = received[:, block, tokens : 2 * tokens, :].reshape(length, E)
        value_rows = received[:, block, 2 * tokens : 3 * tokens, :].reshape(length, E)
        scores = lax.dot_general(
            query_rows, key_rows, (((1,), (1,)), ((), ())), preferred_element_type=F32
        )
        weights = jnp.where(column[:, :1] >= row, scores * key_weight, 0.0).astype(BF)
        out[block] = jnp.dot(weights, value_rows, preferred_element_type=F32) * weight
        query_weights = jnp.where(lane == block, weight * prior_weight, query_weights)
    query_weight[...] = query_weights


def finish(tokens, constants, received, prior, sums, query_weight, out):
    groups, blocks = received.shape[:2]
    scaling = constants[1][:1]
    for block in range(blocks):
        query_rows = received[:, block, :tokens, :].reshape(groups * tokens, E)
        rows = slice(block * ROW, (block + 1) * ROW)
        state = jnp.concatenate(
            [prior[at].astype(F32)[rows] for at in range(prior.shape[0])], axis=0
        ).astype(BF)
        combined = jnp.dot(query_rows, state, preferred_element_type=F32)
        combined = sums[block] + combined * query_weight[:, block : block + 1]
        square = jnp.mean(combined * combined, axis=-1, keepdims=True)
        normal = (combined * lax.rsqrt(square + 1e-06) * scaling).astype(BF)
        out[:, block] = normal.reshape(groups, tokens, E)


def unpack(received, out, sem):
    heads, tokens = received.shape[:2]
    for head in range(heads):
        columns = out.at[0, :, pl.ds(head * E, E)]
        pltpu.make_async_copy(received.at[head], columns, sem).start()
    pltpu.make_async_copy(received, received, sem).wait()


def on_device(query, keys, values, decay_exp, gain, route):
    groups = lax.axis_size("group")
    rows = lax.axis_size("x")
    tokens, width = query.shape[1:]
    heads = decay_exp.shape[0]
    pieces = tokens // ROW
    length = tokens * groups
    scale = 1.0 / (4.0 * length * rows * Z)
    sent_rows = 3 * tokens + ROW
    parts = 4
    sent = pl.pallas_call(
        functools.partial(pack, tokens, pieces),
        in_specs=[anywhere()] * 4,
        out_specs=anywhere(),
        out_shape=jax.ShapeDtypeStruct((heads, sent_rows, E), BF),
        scratch_shapes=[
            pltpu.VMEM((heads, sent_rows, E), BF),
            pltpu.SMEM(route.shape, jnp.int32),
            pltpu.SemaphoreType.DMA((parts,)),
            pltpu.SemaphoreType.DMA((parts,)),
            pltpu.SemaphoreType.DMA,
        ],
        compiler_params=params(62),
        name="pack",
    )(route, query, keys, values)
    received = lax.all_to_all(sent, ("group", "x"), split_axis=0, concat_axis=0, tiled=True)
    received = received.reshape(groups, rows, sent_rows, E)
    sliced, constants = pl.pallas_call(
        functools.partial(states, tokens, scale),
        in_specs=[smem(), vmem(), vmem()],
        out_specs=(vmem(), vmem()),
        out_shape=(
            jax.ShapeDtypeStruct((Z, rows * ROW, E), BF),
            jax.ShapeDtypeStruct((2, ROW, E), F32),
        ),
        compiler_params=params(),
        name="states",
    )(decay_exp, gain.reshape(heads, E), received)
    sliced = lax.all_to_all(sliced, "z", split_axis=0, concat_axis=0, tiled=True)
    priors = pl.pallas_call(
        functools.partial(scan, length),
        in_specs=[vmem(), vmem()],
        out_specs=vmem(),
        out_shape=jax.ShapeDtypeStruct((Z, rows * ROW, E), BF),
        compiler_params=params(),
        name="scan",
    )(constants, sliced)
    priors = lax.all_to_all(priors, "z", split_axis=0, concat_axis=0, tiled=True)
    sums, query_weight = pl.pallas_call(
        functools.partial(within, tokens),
        in_specs=[vmem(), vmem()],
        out_specs=(vmem(), vmem()),
        out_shape=(
            jax.ShapeDtypeStruct((rows, length, E), F32),
            jax.ShapeDtypeStruct((length, E), F32),
        ),
        compiler_params=params(),
        cost_estimate=pl.CostEstimate(
            flops=4 * rows * length * length * E,
            bytes_accessed=4 * rows * length * E * 4,
            transcendentals=rows * length * E,
        ),
        name="within",
    )(constants, received)
    mixed = pl.pallas_call(
        functools.partial(finish, tokens),
        in_specs=[vmem()] * 5,
        out_specs=vmem(),
        out_shape=jax.ShapeDtypeStruct((groups, rows, tokens, E), BF),
        compiler_params=params(),
        name="finish",
    )(constants, received, priors, sums, query_weight)
    mixed = mixed.reshape(heads, tokens, E)
    mixed = lax.all_to_all(mixed, ("group", "x"), split_axis=0, concat_axis=0, tiled=True)
    return pl.pallas_call(
        unpack,
        in_specs=[anywhere()],
        out_specs=anywhere(),
        out_shape=jax.ShapeDtypeStruct((1, tokens, width), BF),
        scratch_shapes=[pltpu.SemaphoreType.DMA],
        compiler_params=params(),
        name="unpack",
    )(mixed)


def solution(mesh):
    devices = np.asarray(mesh.devices)
    split = Mesh(devices.reshape(devices.shape[0], -1, Z), ("group", "x", "z"))
    ctx = ("x", "z")
    stored = P("group", ctx, None)
    in_specs = (stored, stored, stored, P(), P(), P(None, ctx, None))
    return jax.shard_map(
        on_device, mesh=split, in_specs=in_specs, out_specs=stored, check_vma=False
    )
```

time: 108 us -> 101 us (0.935)
  blocking collectives: 95 us -> 77.5 us
  waiting for transfers between devices: 0 us -> 10.2 us
  starting transfers between devices: 0 us -> 5.92 us
  local copies, waits for them, and re-layouts: 3.79 us -> 0.01 us
  other arithmetic: 1.41 us -> 0 us
    all_to_all x1 -> x0, blocking collectives: 17.7 us -> none  [on_device(): lax.all_to_all(priors, 'z', split_axis=0, concat_axis=0, tiled=True)]
    all_to_all x0 -> x1, waiting for transfers between devices: none -> 10.2 us  [on_device(): lax.all_to_all(priors, 'z', split_axis=0, concat_axis=0, tiled=True)]
    all_to_all x0 -> x1, starting transfers between devices: none -> 5.92 us  [on_device(): lax.all_to_all(priors, 'z', split_axis=0, concat_axis=0, tiled=True)]
    unnamed x11 -> x4, local copies, waits for them, and re-layouts: 3.71 us -> 0.01 us
    unnamed x1 -> x0, other arithmetic: 1.33 us -> none
    pallas_call x4 -> x5, Pallas kernels: 5.71 us -> 6.43 us  [the longest x1 2.24 us: on_device(): pl.pallas_call(functools.partial(pack, tokens, pieces), in_specs=[anywher...]
  transfers between devices with their start and end apart: 0 -> 1, of which waited for: 0 -> 1; matrix products, arithmetic and copies ran while one was open for 0% -> 0% of each run, Pallas kernels for 0% -> 2%
where the time goes in v2:
time: 101 us
  blocking collectives  77.5 us (77%)
  waiting for transfers between devices  10.2 us (10%)
  Pallas kernels  7.32 us (7%)
  starting transfers between devices  5.92 us (6%)
    all_to_all x1, blocking collectives, on_device(): lax.all_to_all(sent, ('group', 'x'), split_axis=0, concat_axis=0, tiled=T...  33.8 us
    all_to_all x1, blocking collectives, on_device(): lax.all_to_all(sliced, 'z', split_axis=0, concat_axis=0, tiled=True)  24.7 us
    all_to_all x1, blocking collectives, on_device(): lax.all_to_all(mixed, ('group', 'x'), split_axis=0, concat_axis=0, tiled=...  19 us
    all_to_all x1, waiting for transfers between devices, on_device(): lax.all_to_all(priors, 'z', split_axis=0, concat_axis=0, tiled=True)  10.2 us
    all_to_all x1, starting transfers between devices, on_device(): lax.all_to_all(priors, 'z', split_axis=0, concat_axis=0, tiled=True)  5.92 us
    pallas_call x1, Pallas kernels, on_device(): pl.pallas_call(functools.partial(pack, tokens, pieces), in_specs=[anywher...  2.24 us
  transfers between devices with their start and end apart: 1, of which 1 were waited for; matrix products, arithmetic and copies ran while one was open for 0% of the time, Pallas kernels for 2%

profile of v2, /device:TPU:1, one launch (start us, length us, event | category | flops | bytes accessed | tf_op | source)
XLA Modules:
  0.0 101.0 jit_solution(4847497181267215558)
XLA Ops:
  0.0 2.2 %pack.1 = bf16[32,200,128]{2,1,0:T(8,128)(2,1)} custom-call(s32[8,1,8]{2,1,0:T(1,128)} %route.1, bf16[1,64,4096]{2,1,0:T(8,128)(2,1)} %query.1, bf16[1,64,4096]{2,1,0:T(8,128)(2,1)} %keys.1, bf16[1,64,4096]{2,1,0:T(8,128)(2,1)} %values.1), custom_call_target="tpu_custom_call" | custom-call | tf_op jit(solution)/shard_map/pack/pallas_call | solution.py:187
  2.3 0.0 copy-start
  2.3 0.0 copy-start.1
  2.3 33.8 %all_to_all.20 = bf16[32,200,128]{2,1,0:T(8,128)(2,1)S(1)} all-to-all(bf16[32,200,128]{2,1,0:T(8,128)(2,1)} %pack.1), channel_id=1, replica_groups=mesh['group'=8,'x'=4,'z'=16] {'group','x'}, dimensions={0} | all-to-all | bytes 3276800 | tf_op jit(solution)/shard_map/all_to_all | solution.py:202
  36.1 0.0 copy-done
  36.1 0.0 copy-done.1
  36.1 0.9 states.1
  37.0 24.7 %all_to_all.21.pieces = bf16[16,32,128]{2,1,0:T(8,128)(2,1)S(1)} all-to-all(bf16[16,32,128]{2,1,0:T(8,128)(2,1)S(1)} %get-tuple-element.10), channel_id=1, replica_groups=mesh['group'=8,'x'=4,'z'=16] {'z'}, dimensions={0} | all-to-all | bytes 262144 | tf_op jit(solution)/shard_map/all_to_all | solution.py:215
  61.7 0.8 scan.1
  62.5 5.9 %all-to-all-start.2 = ((bf16[16,32,128]{2,1,0:T(8,128)(2,1)}), bf16[16,32,128]{2,1,0:T(8,128)(2,1)S(1)}, u32[]{:S(2)}, u32[]{:S(2)}) async-start(bf16[16,32,128]{2,1,0:T(8,128)(2,1)} %scan.1), calls=%async_computation.2 | async-start | bytes 262144 | tf_op jit(solution)/shard_map/all_to_all | solution.py:224
  68.4 1.8 %within.1 = (f32[4,512,128]{2,1,0:T(8,128)S(1)}, f32[512,128]{1,0:T(8,128)S(1)}) custom-call(f32[2,8,128]{2,1,0:T(8,128)S(1)} %get-tuple-element.9.constants, bf16[8,4,200,128]{3,2,1,0:T(8,128)(2,1)S(1)} %bitcast.4), custom_call_target="tpu_custom_call" | custom-call | flops 536870912 | bytes 4194304 | tf_op jit(solution)/shard_map/within/pallas_call | solution.py:225
  70.2 10.2 %all-to-all-done.2.prior = bf16[16,32,128]{2,1,0:T(8,128)(2,1)S(1)} async-done(((bf16[16,32,128]{2,1,0:T(8,128)(2,1)}), bf16[16,32,128]{2,1,0:T(8,128)(2,1)S(1)}, u32[]{:S(2)}, u32[]{:S(2)}) %all-to-all-start.2) | async-done | bytes 131104 | tf_op jit(solution)/shard_map/all_to_all | solution.py:224
  80.4 0.9 finish.1
  81.2 19.0 %all_to_all.22.received = bf16[32,64,128]{2,1,0:T(8,128)(2,1)S(1)} all-to-all(bf16[32,64,128]{2,1,0:T(8,128)(2,1)S(1)} %bitcast.6), channel_id=1, replica_groups=mesh['group'=8,'x'=4,'z'=16] {'group','x'}, dimensions={0} | all-to-all | bytes 1048576 | tf_op jit(solution)/shard_map/all_to_all | solution.py:250
  100.2 0.8 unpack.1
Async XLA Ops:
  2.3 33.8 %copy-start = (f32[4096]{0:T(1024)S(1)}, f32[4096]{0:T(1024)}, u32[]{:S(2)}) copy-start(f32[4096]{0:T(1024)} %param.10) | copy-start | bytes 49156
  2.3 33.8 %copy-start.1 = (s32[32]{0:T(128)S(1)}, s32[32]{0:T(128)}, u32[]{:S(2)}) copy-start(s32[32]{0:T(128)} %exp_ref.1) | copy-start | bytes 388
  62.5 17.9 %all-to-all-start.2 = ((bf16[16,32,128]{2,1,0:T(8,128)(2,1)}), bf16[16,32,128]{2,1,0:T(8,128)(2,1)S(1)}, u32[]{:S(2)}, u32[]{:S(2)}) async-start(bf16[16,32,128]{2,1,0:T(8,128)(2,1)} %scan.1), calls=%async_computation.2 | async-start | bytes 262144 | tf_op jit(solution)/shard_map/all_to_all | solution.py:224

commit v3 on v2

--- a/solution.py
+++ b/solution.py
@@ -20,16 +20,8 @@
     return pl.BlockSpec(memory_space=pltpu.VMEM)
 
 
-def smem():
-    return pl.BlockSpec(memory_space=pltpu.SMEM)
-
-
 def params(mebibytes=48):
     return pltpu.CompilerParams(vmem_limit_bytes=mebibytes * 1024 * 1024)
-
-
-def my_head():
-    return lax.axis_index("group") * lax.axis_size("x") + lax.axis_index("x")
 
 
 def anywhere():
@@ -87,11 +79,14 @@
     )
 
 
-def states(tokens, scale, exp_ref, gain, received, out, constants):
+def states(tokens, scale, exponents, gain, received, out, constants):
     groups, blocks = received.shape[:2]
     length = groups * tokens
-    head = my_head()
-    exponent = jnp.full((ROW, E), exp_ref[head], jnp.int32).astype(F32)
+    heads = exponents.shape[1]
+    head = lax.axis_index("group") * lax.axis_size("x") + lax.axis_index("x")
+    mine = lax.broadcasted_iota(jnp.int32, (1, heads), 1) == head
+    exponent = jnp.sum(jnp.where(mine, exponents[...], 0).astype(F32), axis=1, keepdims=True)
+    exponent = jnp.broadcast_to(exponent, (ROW, E))
     decay = jnp.exp2(exponent * exponent / 8.0) * scale
     constants[0] = decay
     constants[1] = jnp.broadcast_to(gain[pl.ds(head, 1), :], (ROW, E))
@@ -112,16 +107,24 @@
 
 def scan(length, constants, pieces, out):
     steps, rows = pieces.shape[:2]
+    blocks = rows // ROW
     decay = jnp.exp(-constants[0] * length)
-    total = jnp.zeros((ROW, E), F32)
-    priors = [[None] * (rows // ROW) for _ in range(steps)]
-    loaded = [pieces[step].astype(F32) for step in range(steps)]
-    for block in range(rows // ROW):
-        for step in range(steps):
-            priors[step][block] = total
-            total = total * decay + loaded[step][block * ROW : (block + 1) * ROW]
+    decays = jnp.concatenate([decay] * blocks, axis=0)
+    total = jnp.zeros((rows, E), F32)
+    priors = []
     for step in range(steps):
-        out[step] = jnp.concatenate(priors[step], axis=0).astype(BF)
+        priors.append(total)
+        total = total * decays + pieces[step].astype(F32)
+    whole = jnp.exp(-constants[0] * (length * steps))
+    carry = jnp.zeros((ROW, E), F32)
+    carries = []
+    for block in range(blocks):
+        carries.append(carry)
+        carry = carry * whole + total[block * ROW : (block + 1) * ROW]
+    carry = jnp.concatenate(carries, axis=0)
+    for step in range(steps):
+        out[step] = (priors[step] + carry).astype(BF)
+        carry = carry * decays
 
 
 def within(tokens, constants, received, out, query_weight):
@@ -153,6 +156,7 @@
 def finish(tokens, constants, received, prior, sums, query_weight, out):
     groups, blocks = received.shape[:2]
     scaling = constants[1][:1]
+    ones = jnp.full((E, E), 1.0 / E, BF)
     for block in range(blocks):
         query_rows = received[:, block, :tokens, :].reshape(groups * tokens, E)
         rows = slice(block * ROW, (block + 1) * ROW)
@@ -161,7 +165,9 @@
         ).astype(BF)
         combined = jnp.dot(query_rows, state, preferred_element_type=F32)
         combined = sums[block] + combined * query_weight[:, block : block + 1]
-        square = jnp.mean(combined * combined, axis=-1, keepdims=True)
+        square = jnp.dot(
+            (combined * combined).astype(BF), ones, preferred_element_type=F32
+        )
         normal = (combined * lax.rsqrt(square + 1e-06) * scaling).astype(BF)
         out[:, block] = normal.reshape(groups, tokens, E)
 
@@ -203,7 +209,7 @@
     received = received.reshape(groups, rows, sent_rows, E)
     sliced, constants = pl.pallas_call(
         functools.partial(states, tokens, scale),
-        in_specs=[smem(), vmem(), vmem()],
+        in_specs=[vmem(), vmem(), vmem()],
         out_specs=(vmem(), vmem()),
         out_shape=(
             jax.ShapeDtypeStruct((Z, rows * ROW, E), BF),
@@ -211,7 +217,7 @@
         ),
         compiler_params=params(),
         name="states",
-    )(decay_exp, gain.reshape(heads, E), received)
+    )(decay_exp.reshape(1, heads), gain.reshape(heads, E), received)
     sliced = lax.all_to_all(sliced, "z", split_axis=0, concat_axis=0, tiled=True)
     priors = pl.pallas_call(
         functools.partial(scan, length),

time: 101 us -> 101 us (level)
  no operation moved by 1% of the time
where the time goes in v3:
time: 101 us; the launch traced here: 100 us
  blocking collectives  77.5 us (77%)
  waiting for transfers between devices  10.2 us (10%)
  Pallas kernels  6.45 us (6%)
  starting transfers between devices  5.92 us (6%)
    all_to_all x1, blocking collectives, on_device(): lax.all_to_all(sent, ('group', 'x'), split_axis=0, concat_axis=0, tiled=T...  33.8 us
    all_to_all x1, blocking collectives, on_device(): lax.all_to_all(sliced, 'z', split_axis=0, concat_axis=0, tiled=True)  24.7 us
    all_to_all x1, blocking collectives, on_device(): lax.all_to_all(mixed, ('group', 'x'), split_axis=0, concat_axis=0, tiled=...  19 us
    all_to_all x1, waiting for transfers between devices, on_device(): lax.all_to_all(priors, 'z', split_axis=0, concat_axis=0, tiled=True)  10.2 us
    all_to_all x1, starting transfers between devices, on_device(): lax.all_to_all(priors, 'z', split_axis=0, concat_axis=0, tiled=True)  5.92 us
    pallas_call x1, Pallas kernels, on_device(): pl.pallas_call(functools.partial(pack, tokens, pieces), in_specs=[anywher...  2.24 us
  transfers between devices with their start and end apart: 1, of which 1 were waited for; matrix products, arithmetic and copies ran while one was open for 0% of the time, Pallas kernels for 2%

profile of v3, /device:TPU:1, one launch (start us, length us, event | category | flops | bytes accessed | tf_op | source)
XLA Modules:
  0.0 100.2 jit_solution(16178323092962009619)
XLA Ops:
  0.0 2.2 %pack.1 = bf16[32,200,128]{2,1,0:T(8,128)(2,1)} custom-call(s32[8,1,8]{2,1,0:T(1,128)} %route.1, bf16[1,64,4096]{2,1,0:T(8,128)(2,1)} %query.1, bf16[1,64,4096]{2,1,0:T(8,128)(2,1)} %keys.1, bf16[1,64,4096]{2,1,0:T(8,128)(2,1)} %values.1), custom_call_target="tpu_custom_call" | custom-call | tf_op jit(solution)/shard_map/pack/pallas_call | solution.py:193
  2.3 0.0 copy-start
  2.3 0.0 copy-start.1
  2.3 33.8 %all_to_all.20 = bf16[32,200,128]{2,1,0:T(8,128)(2,1)S(1)} all-to-all(bf16[32,200,128]{2,1,0:T(8,128)(2,1)} %pack.1), channel_id=1, replica_groups=mesh['group'=8,'x'=4,'z'=16] {'group','x'}, dimensions={0} | all-to-all | bytes 3276800 | tf_op jit(solution)/shard_map/all_to_all | solution.py:208
  36.1 0.0 copy-done
  36.1 0.0 copy-done.1
  36.1 0.4 states.1
  36.5 24.7 %all_to_all.21.pieces = bf16[16,32,128]{2,1,0:T(8,128)(2,1)S(1)} all-to-all(bf16[16,32,128]{2,1,0:T(8,128)(2,1)S(1)} %get-tuple-element.10), channel_id=1, replica_groups=mesh['group'=8,'x'=4,'z'=16] {'z'}, dimensions={0} | all-to-all | bytes 262144 | tf_op jit(solution)/shard_map/all_to_all | solution.py:221
  61.2 0.7 scan.1
  61.9 5.9 %all-to-all-start.2 = ((bf16[16,32,128]{2,1,0:T(8,128)(2,1)}), bf16[16,32,128]{2,1,0:T(8,128)(2,1)S(1)}, u32[]{:S(2)}, u32[]{:S(2)}) async-start(bf16[16,32,128]{2,1,0:T(8,128)(2,1)} %scan.1), calls=%async_computation.2 | async-start | bytes 262144 | tf_op jit(solution)/shard_map/all_to_all | solution.py:230
  67.8 1.8 %within.1 = (f32[4,512,128]{2,1,0:T(8,128)S(1)}, f32[512,128]{1,0:T(8,128)S(1)}) custom-call(f32[2,8,128]{2,1,0:T(8,128)S(1)} %get-tuple-element.9.constants, bf16[8,4,200,128]{3,2,1,0:T(8,128)(2,1)S(1)} %bitcast.5), custom_call_target="tpu_custom_call" | custom-call | flops 536870912 | bytes 4194304 | tf_op jit(solution)/shard_map/within/pallas_call | solution.py:231
  69.6 10.2 %all-to-all-done.2.prior = bf16[16,32,128]{2,1,0:T(8,128)(2,1)S(1)} async-done(((bf16[16,32,128]{2,1,0:T(8,128)(2,1)}), bf16[16,32,128]{2,1,0:T(8,128)(2,1)S(1)}, u32[]{:S(2)}, u32[]{:S(2)}) %all-to-all-start.2) | async-done | bytes 131104 | tf_op jit(solution)/shard_map/all_to_all | solution.py:230
  79.8 0.6 finish.1
  80.4 19.0 %all_to_all.22.received = bf16[32,64,128]{2,1,0:T(8,128)(2,1)S(1)} all-to-all(bf16[32,64,128]{2,1,0:T(8,128)(2,1)S(1)} %bitcast.7), channel_id=1, replica_groups=mesh['group'=8,'x'=4,'z'=16] {'group','x'}, dimensions={0} | all-to-all | bytes 1048576 | tf_op jit(solution)/shard_map/all_to_all | solution.py:256
  99.4 0.8 unpack.1
Async XLA Ops:
  2.3 33.8 %copy-start = (f32[4096]{0:T(1024)S(1)}, f32[4096]{0:T(1024)}, u32[]{:S(2)}) copy-start(f32[4096]{0:T(1024)} %param.10) | copy-start | bytes 49156
  2.3 33.8 %copy-start.1 = (s32[32]{0:T(128)S(1)}, s32[32]{0:T(128)}, u32[]{:S(2)}) copy-start(s32[32]{0:T(128)} %param.9) | copy-start | bytes 388
  61.9 17.9 %all-to-all-start.2 = ((bf16[16,32,128]{2,1,0:T(8,128)(2,1)}), bf16[16,32,128]{2,1,0:T(8,128)(2,1)S(1)}, u32[]{:S(2)}, u32[]{:S(2)}) async-start(bf16[16,32,128]{2,1,0:T(8,128)(2,1)} %scan.1), calls=%async_computation.2 | async-start | bytes 262144 | tf_op jit(solution)/shard_map/all_to_all | solution.py:230

commit v4 on v3

--- a/solution.py
+++ b/solution.py
@@ -11,7 +11,9 @@
 
 BF = jnp.bfloat16
 F32 = jnp.float32
-Z = 16
+QUADS = 4
+QUAD = 4
+FIRST_GROUP, FIRST_X, FIRST_QUAD, FIRST_BEFORE, FIRST_AFTER = 6, 2, 2, 0, 3
 E = 128
 ROW = 8
 
@@ -30,6 +32,7 @@
 
 def pack(tokens, pieces, route, query, keys, values, out, staged, route_ref, in_sems, out_sems, sem):
     heads = out.shape[0]
+    first = FIRST_GROUP * lax.axis_size("x") + FIRST_X
     parts = in_sems.shape[0]
     fetch = pltpu.make_async_copy(route, route_ref, sem)
     fetch.start()
@@ -38,7 +41,7 @@
         for head in range(part * span, (part + 1) * span):
             for at, source in enumerate((query, keys, values)):
                 pltpu.make_async_copy(
-                    source.at[0, :, pl.ds(head * E, E)],
+                    source.at[0, :, pl.ds((head ^ first) * E, E)],
                     staged.at[head, pl.ds(at * tokens, tokens), :],
                     in_sems.at[part],
                 ).start()
@@ -100,31 +103,42 @@
         value_rows = received[:, block, 2 * tokens : 3 * tokens, :].reshape(length, E)
         weighted = (jnp.transpose(key_rows).astype(F32) * weight).astype(BF)
         found.append(jnp.dot(weighted, value_rows, preferred_element_type=F32))
+    span = E // out.shape[0]
     for at in range(out.shape[0]):
-        rows = slice(at * ROW, (at + 1) * ROW)
-        out[at] = jnp.concatenate([state[rows] for state in found], axis=0).astype(BF)
-
-
-def scan(length, constants, pieces, out):
-    steps, rows = pieces.shape[:2]
-    blocks = rows // ROW
-    decay = jnp.exp(-constants[0] * length)
-    decays = jnp.concatenate([decay] * blocks, axis=0)
-    total = jnp.zeros((rows, E), F32)
-    priors = []
+        rows = slice(at * span, (at + 1) * span)
+        out[at] = jnp.concatenate(
+            [found[row ^ FIRST_X][rows] for row in range(blocks)], axis=0
+        ).astype(BF)
+
+
+def totals(length, constants, pieces, out):
+    decay = jnp.exp(-constants[0][:1] * length)
+    total = pieces[FIRST_BEFORE].astype(F32)
+    for step in range(1, pieces.shape[0]):
+        total = total * decay + pieces[step ^ FIRST_BEFORE].astype(F32)
+    total = total.astype(BF)
+    for quad in range(out.shape[0]):
+        out[quad] = total
+
+
+def scan(length, rows, constants, pieces, sums, out):
+    steps = pieces.shape[0]
+    span = pieces.shape[1] // rows
+    decay = jnp.exp(-constants[0][:1] * length)
+    whole = jnp.exp(-constants[0][:1] * (length * steps))
+    mine = lax.axis_index("q")
+    carry = jnp.zeros((span, E), F32)
+    carries = []
+    for row in range(rows):
+        for quad in range(sums.shape[0]):
+            chosen = carry if quad == 0 else jnp.where(mine == quad, carry, chosen)
+            some = sums[quad ^ FIRST_QUAD, row * span : (row + 1) * span, :]
+            carry = carry * whole + some.astype(F32)
+        carries.append(chosen)
+    total = jnp.concatenate(carries, axis=0)
     for step in range(steps):
-        priors.append(total)
-        total = total * decays + pieces[step].astype(F32)
-    whole = jnp.exp(-constants[0] * (length * steps))
-    carry = jnp.zeros((ROW, E), F32)
-    carries = []
-    for block in range(blocks):
-        carries.append(carry)
-        carry = carry * whole + total[block * ROW : (block + 1) * ROW]
-    carry = jnp.concatenate(carries, axis=0)
-    for step in range(steps):
-        out[step] = (priors[step] + carry).astype(BF)
-        carry = carry * decays
+        out[step ^ FIRST_AFTER] = total.astype(BF)
+        total = total * decay + pieces[step ^ FIRST_BEFORE].astype(F32)
 
 
 def within(tokens, constants, received, out, query_weight):
@@ -159,10 +173,12 @@
     ones = jnp.full((E, E), 1.0 / E, BF)
     for block in range(blocks):
         query_rows = received[:, block, :tokens, :].reshape(groups * tokens, E)
-        rows = slice(block * ROW, (block + 1) * ROW)
+        span = prior.shape[1] // blocks
+        row = block ^ FIRST_X
+        slots = [at ^ FIRST_BEFORE ^ FIRST_AFTER for at in range(prior.shape[0])]
         state = jnp.concatenate(
-            [prior[at].astype(F32)[rows] for at in range(prior.shape[0])], axis=0
-        ).astype(BF)
+            [prior[slot, row * span : (row + 1) * span, :] for slot in slots], axis=0
+        )
         combined = jnp.dot(query_rows, state, preferred_element_type=F32)
         combined = sums[block] + combined * query_weight[:, block : block + 1]
         square = jnp.dot(
@@ -173,11 +189,18 @@
 
 
 def unpack(received, out, sem):
-    heads, tokens = received.shape[:2]
-    for head in range(heads):
-        columns = out.at[0, :, pl.ds(head * E, E)]
-        pltpu.make_async_copy(received.at[head], columns, sem).start()
+    first = FIRST_GROUP * lax.axis_size("x") + FIRST_X
+    for slot in range(received.shape[0]):
+        columns = out.at[0, :, pl.ds((slot ^ first) * E, E)]
+        pltpu.make_async_copy(received.at[slot], columns, sem).start()
     pltpu.make_async_copy(received, received, sem).wait()
+
+
+def exchange(value, axis, count, first):
+    order = [[at ^ first for at in range(count)]]
+    return lax.all_to_all(
+        value, axis, split_axis=0, concat_axis=0, tiled=True, axis_index_groups=order
+    )
 
 
 def on_device(query, keys, values, decay_exp, gain, route):
@@ -187,7 +210,7 @@
     heads = decay_exp.shape[0]
     pieces = tokens // ROW
     length = tokens * groups
-    scale = 1.0 / (4.0 * length * rows * Z)
+    scale = 1.0 / (4.0 * length * rows * QUADS * QUAD)
     sent_rows = 3 * tokens + ROW
     parts = 4
     sent = pl.pallas_call(
@@ -205,29 +228,31 @@
         compiler_params=params(62),
         name="pack",
     )(route, query, keys, values)
-    received = lax.all_to_all(sent, ("group", "x"), split_axis=0, concat_axis=0, tiled=True)
+    plane = ("group", "x")
+    first = FIRST_GROUP * rows + FIRST_X
+    received = exchange(sent, plane, heads, first)
     received = received.reshape(groups, rows, sent_rows, E)
     sliced, constants = pl.pallas_call(
         functools.partial(states, tokens, scale),
         in_specs=[vmem(), vmem(), vmem()],
         out_specs=(vmem(), vmem()),
         out_shape=(
-            jax.ShapeDtypeStruct((Z, rows * ROW, E), BF),
+            jax.ShapeDtypeStruct((QUAD, rows * E // QUAD, E), BF),
             jax.ShapeDtypeStruct((2, ROW, E), F32),
         ),
         compiler_params=params(),
         name="states",
     )(decay_exp.reshape(1, heads), gain.reshape(heads, E), received)
-    sliced = lax.all_to_all(sliced, "z", split_axis=0, concat_axis=0, tiled=True)
-    priors = pl.pallas_call(
-        functools.partial(scan, length),
+    sliced = exchange(sliced, "r", QUAD, FIRST_BEFORE)
+    quads = pl.pallas_call(
+        functools.partial(totals, length),
         in_specs=[vmem(), vmem()],
         out_specs=vmem(),
-        out_shape=jax.ShapeDtypeStruct((Z, rows * ROW, E), BF),
-        compiler_params=params(),
-        name="scan",
+        out_shape=jax.ShapeDtypeStruct((QUADS, rows * E // QUAD, E), BF),
+        compiler_params=params(),
+        name="totals",
     )(constants, sliced)
-    priors = lax.all_to_all(priors, "z", split_axis=0, concat_axis=0, tiled=True)
+    quads = exchange(quads, "q", QUADS, FIRST_QUAD)
     sums, query_weight = pl.pallas_call(
         functools.partial(within, tokens),
         in_specs=[vmem(), vmem()],
@@ -244,6 +269,16 @@
         ),
         name="within",
     )(constants, received)
+    quads, sums, query_weight = lax.optimization_barrier((quads, sums, query_weight))
+    priors = pl.pallas_call(
+        functools.partial(scan, length, rows),
+        in_specs=[vmem(), vmem(), vmem()],
+        out_specs=vmem(),
+        out_shape=jax.ShapeDtypeStruct((QUAD, rows * E // QUAD, E), BF),
+        compiler_params=params(),
+        name="scan",
+    )(constants, sliced, quads)
+    priors = exchange(priors, "r", QUAD, FIRST_AFTER)
     mixed = pl.pallas_call(
         functools.partial(finish, tokens),
         in_specs=[vmem()] * 5,
@@ -253,7 +288,7 @@
         name="finish",
     )(constants, received, priors, sums, query_weight)
     mixed = mixed.reshape(heads, tokens, E)
-    mixed = lax.all_to_all(mixed, ("group", "x"), split_axis=0, concat_axis=0, tiled=True)
+    mixed = exchange(mixed, plane, heads, first)
     return pl.pallas_call(
         unpack,
         in_specs=[anywhere()],
@@ -267,8 +302,10 @@
 
 def solution(mesh):
     devices = np.asarray(mesh.devices)
-    split = Mesh(devices.reshape(devices.shape[0], -1, Z), ("group", "x", "z"))
-    ctx = ("x", "z")
+    split = Mesh(
+        devices.reshape(devices.shape[0], -1, QUADS, QUAD), ("group", "x", "q", "r")
+    )
+    ctx = ("x", "q", "r")
     stored = P("group", ctx, None)
     in_specs = (stored, stored, stored, P(), P(), P(None, ctx, None))
     return jax.shard_map(

time: 101 us -> 91.2 us (0.903)
  blocking collectives: 77.5 us -> 68.3 us
  waiting for transfers between devices: 10.2 us -> 2.22 us
  starting transfers between devices: 5.92 us -> 13.5 us
    all_to_all x3 -> x4, blocking collectives: 77.5 us -> 68.3 us  [exchange(): lax.all_to_all(value, axis, split_axis=0, concat_axis=0, tiled=True, axis...]
    all_to_all x1, waiting for transfers between devices: 10.2 us -> 2.22 us  [exchange(): lax.all_to_all(value, axis, split_axis=0, concat_axis=0, tiled=True, axis...]
    all_to_all x1, starting transfers between devices: 5.92 us -> 13.5 us  [exchange(): lax.all_to_all(value, axis, split_axis=0, concat_axis=0, tiled=True, axis...]
where the time goes in v4:
time: 91.2 us; the launch traced here: 90.6 us
  blocking collectives  68.3 us (75%)
  starting transfers between devices  13.5 us (15%)
  Pallas kernels  6.48 us (7%)
  waiting for transfers between devices  2.22 us (2%)
    all_to_all x4, blocking collectives, exchange(): lax.all_to_all(value, axis, split_axis=0, concat_axis=0, tiled=True, axis...  68.3 us
    all_to_all x1, starting transfers between devices, exchange(): lax.all_to_all(value, axis, split_axis=0, concat_axis=0, tiled=True, axis...  13.5 us
    pallas_call x1, Pallas kernels, on_device(): pl.pallas_call(functools.partial(pack, tokens, pieces), in_specs=[anywher...  2.25 us
    all_to_all x1, waiting for transfers between devices, exchange(): lax.all_to_all(value, axis, split_axis=0, concat_axis=0, tiled=True, axis...  2.22 us
  transfers between devices with their start and end apart: 1, of which 1 were waited for; matrix products, arithmetic and copies ran while one was open for 0% of the time, Pallas kernels for 2%

profile of v4, /device:TPU:1, one launch (start us, length us, event | category | flops | bytes accessed | tf_op | source)
XLA Modules:
  0.0 90.6 jit_solution(8083085902676272035)
XLA Ops:
  0.0 2.2 %pack.1 = bf16[32,200,128]{2,1,0:T(8,128)(2,1)} custom-call(s32[8,1,8]{2,1,0:T(1,128)} %route.1, bf16[1,64,4096]{2,1,0:T(8,128)(2,1)} %query.1, bf16[1,64,4096]{2,1,0:T(8,128)(2,1)} %keys.1, bf16[1,64,4096]{2,1,0:T(8,128)(2,1)} %values.1), custom_call_target="tpu_custom_call" | custom-call | tf_op jit(solution)/shard_map/pack/pallas_call | solution.py:216
  2.3 0.0 copy-start
  2.3 0.0 copy-start.1
  2.3 33.4 %all_to_all.25 = bf16[32,200,128]{2,1,0:T(8,128)(2,1)S(1)} all-to-all(bf16[32,200,128]{2,1,0:T(8,128)(2,1)} %pack.1), channel_id=1, replica_groups={{416,432,384,400,480,496,448,464,288,304,256,272,352,368,320,336,160,17..., dimensions={0} | all-to-all | bytes 3276800 | tf_op jit(solution)/shard_map/all_to_all | solution.py:201
  35.7 0.0 copy-done
  35.7 0.0 copy-done.1
  35.7 0.4 states.1
  36.1 7.7 %all_to_all.26.pieces = bf16[4,128,128]{2,1,0:T(8,128)(2,1)S(1)} all-to-all(bf16[4,128,128]{2,1,0:T(8,128)(2,1)S(1)} %get-tuple-element.13), channel_id=1, replica_groups={{0,1,2,3},{4,5,6,7},{8,9,10,11},{12,13,14,15},{16,17,18,19},{20,21,22,2..., dimensions={0} | all-to-all | bytes 262144 | tf_op jit(solution)/shard_map/all_to_all | solution.py:201
  43.8 0.7 totals.1
  44.4 13.5 %all-to-all-start.2 = ((bf16[4,128,128]{2,1,0:T(8,128)(2,1)}), bf16[4,128,128]{2,1,0:T(8,128)(2,1)S(1)}, u32[]{:S(2)}, u32[]{:S(2)}) async-start(bf16[4,128,128]{2,1,0:T(8,128)(2,1)} %totals.1), calls=%async_computation.2 | async-start | bytes 262144 | tf_op jit(solution)/shard_map/all_to_all | solution.py:201
  58.0 1.7 %within.1 = (f32[4,512,128]{2,1,0:T(8,128)S(1)}, f32[512,128]{1,0:T(8,128)S(1)}) custom-call(f32[2,8,128]{2,1,0:T(8,128)S(1)} %get-tuple-element.12.constants, bf16[8,4,200,128]{3,2,1,0:T(8,128)(2,1)S(1)} %bitcast.5), custom_call_target="tpu_custom_call" | custom-call | flops 536870912 | bytes 4194304 | tf_op jit(solution)/shard_map/within/pallas_call | solution.py:256
  59.7 2.2 %all-to-all-done.2.sums = bf16[4,128,128]{2,1,0:T(8,128)(2,1)S(1)} async-done(((bf16[4,128,128]{2,1,0:T(8,128)(2,1)}), bf16[4,128,128]{2,1,0:T(8,128)(2,1)S(1)}, u32[]{:S(2)}, u32[]{:S(2)}) %all-to-all-start.2) | async-done | bytes 131104 | tf_op jit(solution)/shard_map/all_to_all | solution.py:201
  61.9 0.1 scan.1
  62.0 7.2 %all_to_all.27.prior = bf16[4,128,128]{2,1,0:T(8,128)(2,1)S(1)} all-to-all(bf16[4,128,128]{2,1,0:T(8,128)(2,1)S(1)} %scan.1), channel_id=1, replica_groups={{3,2,1,0},{7,6,5,4},{11,10,9,8},{15,14,13,12},{19,18,17,16},{23,22,21,2..., dimensions={0} | all-to-all | bytes 262144 | tf_op jit(solution)/shard_map/all_to_all | solution.py:201
  69.2 0.6 finish.1
  69.8 20.1 %all_to_all.28.received = bf16[32,64,128]{2,1,0:T(8,128)(2,1)S(1)} all-to-all(bf16[32,64,128]{2,1,0:T(8,128)(2,1)S(1)} %bitcast.7), channel_id=1, replica_groups={{416,432,384,400,480,496,448,464,288,304,256,272,352,368,320,336,160,17..., dimensions={0} | all-to-all | bytes 1048576 | tf_op jit(solution)/shard_map/all_to_all | solution.py:201
  89.9 0.8 unpack.1
Async XLA Ops:
  2.3 33.4 %copy-start = (f32[4096]{0:T(1024)S(1)}, f32[4096]{0:T(1024)}, u32[]{:S(2)}) copy-start(f32[4096]{0:T(1024)} %param.10) | copy-start | bytes 49156
  2.3 33.4 %copy-start.1 = (s32[32]{0:T(128)S(1)}, s32[32]{0:T(128)}, u32[]{:S(2)}) copy-start(s32[32]{0:T(128)} %param.9) | copy-start | bytes 388
  44.4 17.5 %all-to-all-start.2 = ((bf16[4,128,128]{2,1,0:T(8,128)(2,1)}), bf16[4,128,128]{2,1,0:T(8,128)(2,1)S(1)}, u32[]{:S(2)}, u32[]{:S(2)}) async-start(bf16[4,128,128]{2,1,0:T(8,128)(2,1)} %totals.1), calls=%async_computation.2 | async-start | bytes 262144 | tf_op jit(solution)/shard_map/all_to_all | solution.py:201

commit v5 on v4

--- a/solution.py
+++ b/solution.py
@@ -13,9 +13,10 @@
 F32 = jnp.float32
 QUADS = 4
 QUAD = 4
-FIRST_GROUP, FIRST_X, FIRST_QUAD, FIRST_BEFORE, FIRST_AFTER = 6, 2, 2, 0, 3
 E = 128
 ROW = 8
+FIRST_GROUP, FIRST_X, FIRST_QUAD, FIRST_BEFORE, FIRST_AFTER = 5, 2, 2, 2, 2
+LAST_GROUP, LAST_X = 5, 2
 
 
 def vmem():
@@ -82,7 +83,26 @@
     )
 
 
-def states(tokens, scale, exponents, gain, received, out, constants):
+def within(tokens, decay, received, block):
+    length = received.shape[0] * tokens
+    middle = length / 2.0
+    chunks = row_positions(received, tokens, block)
+    row = jnp.concatenate([chunk[:1] for chunk in chunks], axis=1)
+    key_weight = jnp.exp(jnp.concatenate([decay] * len(chunks), axis=1) * (row - middle))
+    column = column_positions(chunks)
+    weight = jnp.exp(-decay * (column - middle))
+    query_rows = received[:, block, :tokens, :].reshape(length, E)
+    key_rows = received[:, block, tokens : 2 * tokens, :].reshape(length, E)
+    value_rows = received[:, block, 2 * tokens : 3 * tokens, :].reshape(length, E)
+    scores = lax.dot_general(
+        query_rows, key_rows, (((1,), (1,)), ((), ())), preferred_element_type=F32
+    )
+    weights = jnp.where(column[:, :1] >= row, scores * key_weight, 0.0).astype(BF)
+    sums = jnp.dot(weights, value_rows, preferred_element_type=F32) * weight
+    return sums, weight * jnp.exp(-decay * (middle + 1.0))
+
+
+def states(tokens, scale, exponents, gain, received, out, constants, sums, query_weight):
     groups, blocks = received.shape[:2]
     length = groups * tokens
     heads = exponents.shape[1]
@@ -110,6 +130,15 @@
             [found[row ^ FIRST_X][rows] for row in range(blocks)], axis=0
         ).astype(BF)
 
+    @pl.when(lax.axis_index("q") != FIRST_QUAD)
+    def _():
+        lane = lax.broadcasted_iota(jnp.int32, (length, E), 1)
+        weights = jnp.zeros((length, E), F32)
+        for block in range(blocks):
+            sums[block], weight = within(tokens, decay[:1], received, block)
+            weights = jnp.where(lane == block, weight, weights)
+        query_weight[...] = weights
+
 
 def totals(length, constants, pieces, out):
     decay = jnp.exp(-constants[0][:1] * length)
@@ -141,55 +170,41 @@
         total = total * decay + pieces[step ^ FIRST_BEFORE].astype(F32)
 
 
-def within(tokens, constants, received, out, query_weight):
-    groups, blocks = received.shape[:2]
-    length = groups * tokens
-    middle = length / 2.0
-    decay = constants[0][:1]
-    prior_weight = jnp.exp(-decay * (middle + 1.0))
-    lane = lax.broadcasted_iota(jnp.int32, (length, E), 1)
-    query_weights = jnp.zeros((length, E), F32)
-    for block in range(blocks):
-        chunks = row_positions(received, tokens, block)
-        row = jnp.concatenate([chunk[:1] for chunk in chunks], axis=1)
-        key_weight = jnp.exp(jnp.concatenate([decay] * len(chunks), axis=1) * (row - middle))
-        column = column_positions(chunks)
-        weight = jnp.exp(-decay * (column - middle))
-        query_rows = received[:, block, :tokens, :].reshape(length, E)
-        key_rows = received[:, block, tokens : 2 * tokens, :].reshape(length, E)
-        value_rows = received[:, block, 2 * tokens : 3 * tokens, :].reshape(length, E)
-        scores = lax.dot_general(
-            query_rows, key_rows, (((1,), (1,)), ((), ())), preferred_element_type=F32
-        )
-        weights = jnp.where(column[:, :1] >= row, scores * key_weight, 0.0).astype(BF)
-        out[block] = jnp.dot(weights, value_rows, preferred_element_type=F32) * weight
-        query_weights = jnp.where(lane == block, weight * prior_weight, query_weights)
-    query_weight[...] = query_weights
-
-
 def finish(tokens, constants, received, prior, sums, query_weight, out):
     groups, blocks = received.shape[:2]
-    scaling = constants[1][:1]
+    decay, scaling = constants[0][:1], constants[1][:1]
     ones = jnp.full((E, E), 1.0 / E, BF)
-    for block in range(blocks):
-        query_rows = received[:, block, :tokens, :].reshape(groups * tokens, E)
-        span = prior.shape[1] // blocks
+    span = prior.shape[1] // blocks
+    slots = [at ^ FIRST_BEFORE ^ FIRST_AFTER for at in range(prior.shape[0])]
+
+    def add(block, own, weight):
         row = block ^ FIRST_X
-        slots = [at ^ FIRST_BEFORE ^ FIRST_AFTER for at in range(prior.shape[0])]
         state = jnp.concatenate(
             [prior[slot, row * span : (row + 1) * span, :] for slot in slots], axis=0
         )
-        combined = jnp.dot(query_rows, state, preferred_element_type=F32)
-        combined = sums[block] + combined * query_weight[:, block : block + 1]
+        query_rows = received[:, block, :tokens, :].reshape(groups * tokens, E)
+        combined = own + jnp.dot(query_rows, state, preferred_element_type=F32) * weight
         square = jnp.dot(
             (combined * combined).astype(BF), ones, preferred_element_type=F32
         )
         normal = (combined * lax.rsqrt(square + 1e-06) * scaling).astype(BF)
-        out[:, block] = normal.reshape(groups, tokens, E)
+        for group in range(groups):
+            to = (group ^ FIRST_GROUP ^ LAST_GROUP, row ^ LAST_X)
+            out[to] = normal[group * tokens : (group + 1) * tokens]
+
+    @pl.when(lax.axis_index("q") != FIRST_QUAD)
+    def _():
+        for block in range(blocks):
+            add(block, sums[block], query_weight[:, block : block + 1])
+
+    @pl.when(lax.axis_index("q") == FIRST_QUAD)
+    def _():
+        for block in range(blocks):
+            add(block, *within(tokens, decay, received, block))
 
 
 def unpack(received, out, sem):
-    first = FIRST_GROUP * lax.axis_size("x") + FIRST_X
+    first = LAST_GROUP * lax.axis_size("x") + LAST_X
     for slot in range(received.shape[0]):
         columns = out.at[0, :, pl.ds((slot ^ first) * E, E)]
         pltpu.make_async_copy(received.at[slot], columns, sem).start()
@@ -232,13 +247,15 @@
     first = FIRST_GROUP * rows + FIRST_X
     received = exchange(sent, plane, heads, first)
     received = received.reshape(groups, rows, sent_rows, E)
-    sliced, constants = pl.pallas_call(
+    sliced, constants, sums, query_weight = pl.pallas_call(
         functools.partial(states, tokens, scale),
         in_specs=[vmem(), vmem(), vmem()],
-        out_specs=(vmem(), vmem()),
+        out_specs=(vmem(), vmem(), vmem(), vmem()),
         out_shape=(
             jax.ShapeDtypeStruct((QUAD, rows * E // QUAD, E), BF),
             jax.ShapeDtypeStruct((2, ROW, E), F32),
+            jax.ShapeDtypeStruct((rows, length, E), F32),
+            jax.ShapeDtypeStruct((length, E), F32),
         ),
         compiler_params=params(),
         name="states",
@@ -253,23 +270,6 @@
         name="totals",
     )(constants, sliced)
     quads = exchange(quads, "q", QUADS, FIRST_QUAD)
-    sums, query_weight = pl.pallas_call(
-        functools.partial(within, tokens),
-        in_specs=[vmem(), vmem()],
-        out_specs=(vmem(), vmem()),
-        out_shape=(
-            jax.ShapeDtypeStruct((rows, length, E), F32),
-            jax.ShapeDtypeStruct((length, E), F32),
-        ),
-        compiler_params=params(),
-        cost_estimate=pl.CostEstimate(
-            flops=4 * rows * length * length * E,
-            bytes_accessed=4 * rows * length * E * 4,
-            transcendentals=rows * length * E,
-        ),
-        name="within",
-    )(constants, received)
-    quads, sums, query_weight = lax.optimization_barrier((quads, sums, query_weight))
     priors = pl.pallas_call(
         functools.partial(scan, length, rows),
         in_specs=[vmem(), vmem(), vmem()],
@@ -288,7 +288,7 @@
         name="finish",
     )(constants, received, priors, sums, query_weight)
     mixed = mixed.reshape(heads, tokens, E)
-    mixed = exchange(mixed, plane, heads, first)
+    mixed = exchange(mixed, plane, heads, LAST_GROUP * rows + LAST_X)
     return pl.pallas_call(
         unpack,
         in_specs=[anywhere()],

time: 91.2 us -> 88.7 us (0.973)
  blocking collectives: 68.3 us -> 82.4 us
  starting transfers between devices: 13.5 us -> 0 us
  waiting for transfers between devices: 2.22 us -> 0 us
    all_to_all x4 -> x5, blocking collectives: 68.3 us -> 82.4 us  [exchange(): lax.all_to_all(value, axis, split_axis=0, concat_axis=0, tiled=True, axis...]
    all_to_all x1 -> x0, starting transfers between devices: 13.5 us -> none  [exchange(): lax.all_to_all(value, axis, split_axis=0, concat_axis=0, tiled=True, axis...]
    all_to_all x1 -> x0, waiting for transfers between devices: 2.22 us -> none  [exchange(): lax.all_to_all(value, axis, split_axis=0, concat_axis=0, tiled=True, axis...]
    pallas_call x1, Pallas kernels: 0.38 us -> 2.13 us  [on_device(): pl.pallas_call(functools.partial(states, tokens, scale), in_specs=[vmem()...]
    pallas_call x1 -> x0, Pallas kernels: 1.75 us -> none  [on_device(): pl.pallas_call(functools.partial(within, tokens), in_specs=[vmem(), vmem(...]
  transfers between devices with their start and end apart: 1 -> 0, of which waited for: 1 -> 0; matrix products, arithmetic and copies ran while one was open for 0% -> 0% of each run, Pallas kernels for 2% -> 0%
where the time goes in v5:
time: 88.7 us; the launch traced here: 88.2 us
  blocking collectives  82.4 us (93%)
  Pallas kernels  5.8 us (7%)
    all_to_all x5, blocking collectives, exchange(): lax.all_to_all(value, axis, split_axis=0, concat_axis=0, tiled=True, axis...  82.4 us
    pallas_call x1, Pallas kernels, on_device(): pl.pallas_call(functools.partial(pack, tokens, pieces), in_specs=[anywher...  2.24 us
    pallas_call x1, Pallas kernels, on_device(): pl.pallas_call(functools.partial(states, tokens, scale), in_specs=[vmem()...  2.13 us

profile of v5, /device:TPU:1, one launch (start us, length us, event | category | flops | bytes accessed | tf_op | source)
XLA Modules:
  0.0 88.2 jit_solution(10133321310719919717)
XLA Ops:
  0.0 2.2 %pack.1 = bf16[32,200,128]{2,1,0:T(8,128)(2,1)} custom-call(s32[8,1,8]{2,1,0:T(1,128)} %route.1, bf16[1,64,4096]{2,1,0:T(8,128)(2,1)} %query.1, bf16[1,64,4096]{2,1,0:T(8,128)(2,1)} %keys.1, bf16[1,64,4096]{2,1,0:T(8,128)(2,1)} %values.1), custom_call_target="tpu_custom_call" | custom-call | tf_op jit(solution)/shard_map/pack/pallas_call | solution.py:231
  2.2 0.0 copy-start
  2.3 0.0 copy-start.1
  2.3 32.4 %all_to_all.25 = bf16[32,200,128]{2,1,0:T(8,128)(2,1)S(1)} all-to-all(bf16[32,200,128]{2,1,0:T(8,128)(2,1)} %pack.1), channel_id=1, replica_groups={{352,368,320,336,288,304,256,272,480,496,448,464,416,432,384,400,96,112..., dimensions={0} | all-to-all | bytes 3276800 | tf_op jit(solution)/shard_map/all_to_all | solution.py:216
  34.7 0.0 copy-done
  34.7 0.0 copy-done.1
  34.7 2.1 %states.1 = (bf16[4,128,128]{2,1,0:T(8,128)(2,1)S(1)}, f32[2,8,128]{2,1,0:T(8,128)S(1)}, f32[4,512,128]{2,1,0:T(8,128)S(1)}, f32[512,128]{1,0:T(8,128)S(1)}) custom-call(s32[1,32]{1,0:T(1,128)S(1)} %bitcast.8, f32[32,128]{1,0:T(8,128)S(1)} %bitcast.7, bf16[8,4,200,128]{3,2,1,0:T(8,128)(2,1)S(1)} %bitcast.4), custom_call_target="tpu_custom_call" | custom-call | tf_op jit(solution)/shard_map/states/pallas_call | solution.py:250
  36.9 6.2 %all_to_all.26.pieces = bf16[4,128,128]{2,1,0:T(8,128)(2,1)S(1)} all-to-all(bf16[4,128,128]{2,1,0:T(8,128)(2,1)S(1)} %get-tuple-element.10), channel_id=1, replica_groups={{2,3,0,1},{6,7,4,5},{10,11,8,9},{14,15,12,13},{18,19,16,17},{22,23,20,2..., dimensions={0} | all-to-all | bytes 262144 | tf_op jit(solution)/shard_map/all_to_all | solution.py:216
  43.1 16.1 %all_to_all.27.sums = bf16[4,128,128]{2,1,0:T(8,128)(2,1)S(1)} all-to-all(bf16[4,128,128]{2,1,0:T(8,128)(2,1)S(1)} %totals.1), channel_id=1, replica_groups={{8,12,0,4},{9,13,1,5},{10,14,2,6},{11,15,3,7},{24,28,16,20},{25,29,17,2..., dimensions={0} | all-to-all | bytes 262144 | tf_op jit(solution)/shard_map/all_to_all | solution.py:216
  59.2 0.1 scan.1
  59.3 7.6 %all_to_all.28.prior = bf16[4,128,128]{2,1,0:T(8,128)(2,1)S(1)} all-to-all(bf16[4,128,128]{2,1,0:T(8,128)(2,1)S(1)} %scan.1), channel_id=1, replica_groups={{2,3,0,1},{6,7,4,5},{10,11,8,9},{14,15,12,13},{18,19,16,17},{22,23,20,2..., dimensions={0} | all-to-all | bytes 262144 | tf_op jit(solution)/shard_map/all_to_all | solution.py:216
  66.9 0.6 finish.1
  67.5 20.0 %all_to_all.29.received = bf16[32,64,128]{2,1,0:T(8,128)(2,1)S(1)} all-to-all(bf16[32,64,128]{2,1,0:T(8,128)(2,1)S(1)} %bitcast.6), channel_id=1, replica_groups={{352,368,320,336,288,304,256,272,480,496,448,464,416,432,384,400,96,112..., dimensions={0} | all-to-all | bytes 1048576 | tf_op jit(solution)/shard_map/all_to_all | solution.py:216
  87.5 0.8 unpack.1
  (1 shorter events, 0.0 us)
Async XLA Ops:
  2.2 32.5 %copy-start = (f32[4096]{0:T(1024)S(1)}, f32[4096]{0:T(1024)}, u32[]{:S(2)}) copy-start(f32[4096]{0:T(1024)} %param.10) | copy-start | bytes 49156
  2.3 32.5 %copy-start.1 = (s32[32]{0:T(128)S(1)}, s32[32]{0:T(128)}, u32[]{:S(2)}) copy-start(s32[32]{0:T(128)} %param.9) | copy-start | bytes 388

commit v6 on v5

--- a/solution.py
+++ b/solution.py
@@ -15,8 +15,8 @@
 QUAD = 4
 E = 128
 ROW = 8
-FIRST_GROUP, FIRST_X, FIRST_QUAD, FIRST_BEFORE, FIRST_AFTER = 5, 2, 2, 2, 2
-LAST_GROUP, LAST_X = 5, 2
+FIRST_GROUP, FIRST_X, FIRST_QUAD, FIRST_BEFORE, FIRST_AFTER = 7, 2, 2, 1, 2
+LAST_GROUP, LAST_X = 7, 2
 
 
 def vmem():
@@ -31,21 +31,18 @@
     return pl.BlockSpec(memory_space=pl.ANY)
 
 
-def pack(tokens, pieces, route, query, keys, values, out, staged, route_ref, in_sems, out_sems, sem):
+def pack(tokens, pieces, route, query, keys, values, out, route_ref, in_sems, sem):
     heads = out.shape[0]
     first = FIRST_GROUP * lax.axis_size("x") + FIRST_X
-    parts = in_sems.shape[0]
     fetch = pltpu.make_async_copy(route, route_ref, sem)
     fetch.start()
-    span = heads // parts
-    for part in range(parts):
-        for head in range(part * span, (part + 1) * span):
-            for at, source in enumerate((query, keys, values)):
-                pltpu.make_async_copy(
-                    source.at[0, :, pl.ds((head ^ first) * E, E)],
-                    staged.at[head, pl.ds(at * tokens, tokens), :],
-                    in_sems.at[part],
-                ).start()
+    for at, source in enumerate((query, keys, values)):
+        for slot in range(heads):
+            pltpu.make_async_copy(
+                source.at[0, :, pl.ds((slot ^ first) * E, E)],
+                out.at[slot, pl.ds(at * tokens, tokens), :],
+                in_sems.at[at],
+            ).start()
     token = lax.broadcasted_iota(jnp.int32, (ROW, E), 1) % tokens
     places = jnp.zeros((ROW, E), jnp.int32)
     group = lax.axis_index("group")
@@ -53,17 +50,11 @@
     for piece in range(pieces):
         places = jnp.where(token // ROW == piece, route_ref[group, 0, piece], places)
     places = places.astype(F32).astype(BF)
-    for head in range(heads):
-        staged[head, 3 * tokens :, :] = places
-    copies = []
-    for part in range(parts):
-        some = pl.ds(part * span, span)
-        landed = staged.at[some, pl.ds(0, 3 * tokens), :]
-        pltpu.make_async_copy(landed, landed, in_sems.at[part]).wait()
-        copies.append(pltpu.make_async_copy(staged.at[some], out.at[some], out_sems.at[part]))
-        copies[-1].start()
-    for copy in copies:
-        copy.wait()
+    for slot in range(heads):
+        out[slot, 3 * tokens :, :] = places
+    for at in range(3):
+        landed = out.at[:, pl.ds(at * tokens, tokens), :]
+        pltpu.make_async_copy(landed, landed, in_sems.at[at]).wait()
 
 
 def row_positions(received, tokens, block):
@@ -227,22 +218,19 @@
     length = tokens * groups
     scale = 1.0 / (4.0 * length * rows * QUADS * QUAD)
     sent_rows = 3 * tokens + ROW
-    parts = 4
     sent = pl.pallas_call(
         functools.partial(pack, tokens, pieces),
         in_specs=[anywhere()] * 4,
-        out_specs=anywhere(),
+        out_specs=vmem(),
         out_shape=jax.ShapeDtypeStruct((heads, sent_rows, E), BF),
         scratch_shapes=[
-            pltpu.VMEM((heads, sent_rows, E), BF),
             pltpu.SMEM(route.shape, jnp.int32),
-            pltpu.SemaphoreType.DMA((parts,)),
-            pltpu.SemaphoreType.DMA((parts,)),
+            pltpu.SemaphoreType.DMA((3,)),
             pltpu.SemaphoreType.DMA,
         ],
-        compiler_params=params(62),
+        compiler_params=params(),
         name="pack",
-    )(route, query, keys, values)
+    )(*[pltpu.with_memory_space_constraint(x, pltpu.HBM) for x in (route, query, keys, values)])
     plane = ("group", "x")
     first = FIRST_GROUP * rows + FIRST_X
     received = exchange(sent, plane, heads, first)

time: 88.7 us -> 88.2 us (level)
  no operation moved by 1% of the time
where the time goes in v6:
time: 88.2 us; the launch traced here: 87.8 us
  blocking collectives  82.7 us (94%)
  Pallas kernels  5.03 us (6%)
    all_to_all x5, blocking collectives, exchange(): lax.all_to_all(value, axis, split_axis=0, concat_axis=0, tiled=True, axis...  82.7 us
    pallas_call x1, Pallas kernels, on_device(): pl.pallas_call(functools.partial(states, tokens, scale), in_specs=[vmem()...  2.15 us

profile of v6, /device:TPU:1, one launch (start us, length us, event | category | flops | bytes accessed | tf_op | source)
XLA Modules:
  0.0 87.8 jit_solution(4846228918754103676)
XLA Ops:
  0.0 1.4 %pack.1 = bf16[32,200,128]{2,1,0:T(8,128)(2,1)S(1)} custom-call(s32[8,1,8]{2,1,0:T(1,128)} %route.1, bf16[1,64,4096]{2,1,0:T(8,128)(2,1)} %query.1, bf16[1,64,4096]{2,1,0:T(8,128)(2,1)} %keys.1, bf16[1,64,4096]{2,1,0:T(8,128)(2,1)} %values.1), custom_call_target="tpu_custom_call" | custom-call | tf_op jit(solution)/shard_map/pack/pallas_call | solution.py:221
  1.4 0.0 copy-start
  1.5 0.0 copy-start.1
  1.5 32.6 %all_to_all.25 = bf16[32,200,128]{2,1,0:T(8,128)(2,1)S(1)} all-to-all(bf16[32,200,128]{2,1,0:T(8,128)(2,1)S(1)} %pack.1), channel_id=1, replica_groups={{480,496,448,464,416,432,384,400,352,368,320,336,288,304,256,272,224,24..., dimensions={0} | all-to-all | bytes 3276800 | tf_op jit(solution)/shard_map/all_to_all | solution.py:207
  34.1 0.0 copy-done
  34.1 0.0 copy-done.1
  34.1 2.2 %states.1 = (bf16[4,128,128]{2,1,0:T(8,128)(2,1)S(1)}, f32[2,8,128]{2,1,0:T(8,128)S(1)}, f32[4,512,128]{2,1,0:T(8,128)S(1)}, f32[512,128]{1,0:T(8,128)S(1)}) custom-call(s32[1,32]{1,0:T(1,128)S(1)} %bitcast.8, f32[32,128]{1,0:T(8,128)S(1)} %bitcast.7, bf16[8,4,200,128]{3,2,1,0:T(8,128)(2,1)S(1)} %bitcast.4), custom_call_target="tpu_custom_call" | custom-call | tf_op jit(solution)/shard_map/states/pallas_call | solution.py:238
  36.3 6.5 %all_to_all.26.pieces = bf16[4,128,128]{2,1,0:T(8,128)(2,1)S(1)} all-to-all(bf16[4,128,128]{2,1,0:T(8,128)(2,1)S(1)} %get-tuple-element.10), channel_id=1, replica_groups={{1,0,3,2},{5,4,7,6},{9,8,11,10},{13,12,15,14},{17,16,19,18},{21,20,23,2..., dimensions={0} | all-to-all | bytes 262144 | tf_op jit(solution)/shard_map/all_to_all | solution.py:207
  42.8 16.8 %all_to_all.27.sums = bf16[4,128,128]{2,1,0:T(8,128)(2,1)S(1)} all-to-all(bf16[4,128,128]{2,1,0:T(8,128)(2,1)S(1)} %totals.1), channel_id=1, replica_groups={{8,12,0,4},{9,13,1,5},{10,14,2,6},{11,15,3,7},{24,28,16,20},{25,29,17,2..., dimensions={0} | all-to-all | bytes 262144 | tf_op jit(solution)/shard_map/all_to_all | solution.py:207
  59.6 0.1 scan.1
  59.7 6.3 %all_to_all.28.prior = bf16[4,128,128]{2,1,0:T(8,128)(2,1)S(1)} all-to-all(bf16[4,128,128]{2,1,0:T(8,128)(2,1)S(1)} %scan.1), channel_id=1, replica_groups={{2,3,0,1},{6,7,4,5},{10,11,8,9},{14,15,12,13},{18,19,16,17},{22,23,20,2..., dimensions={0} | all-to-all | bytes 262144 | tf_op jit(solution)/shard_map/all_to_all | solution.py:207
  66.0 0.6 finish.1
  66.6 20.4 %all_to_all.29.received = bf16[32,64,128]{2,1,0:T(8,128)(2,1)S(1)} all-to-all(bf16[32,64,128]{2,1,0:T(8,128)(2,1)S(1)} %bitcast.6), channel_id=1, replica_groups={{480,496,448,464,416,432,384,400,352,368,320,336,288,304,256,272,224,24..., dimensions={0} | all-to-all | bytes 1048576 | tf_op jit(solution)/shard_map/all_to_all | solution.py:207
  87.0 0.8 unpack.1
  (1 shorter events, 0.0 us)
Async XLA Ops:
  1.4 32.7 %copy-start = (f32[4096]{0:T(1024)S(1)}, f32[4096]{0:T(1024)}, u32[]{:S(2)}) copy-start(f32[4096]{0:T(1024)} %param.10) | copy-start | bytes 49156
  1.5 32.6 %copy-start.1 = (s32[32]{0:T(128)S(1)}, s32[32]{0:T(128)}, u32[]{:S(2)}) copy-start(s32[32]{0:T(128)} %param.9) | copy-start | bytes 388

commit v7 on v6

v7 whole, which is shorter than its diff:
```python
import functools

import jax
import jax.numpy as jnp
import numpy as np
from jax import lax
from jax.experimental import pallas as pl
from jax.experimental.pallas import tpu as pltpu
from jax.sharding import Mesh
from jax.sharding import PartitionSpec as P

BF = jnp.bfloat16
F32 = jnp.float32
QUADS = 4
QUAD = 4
E = 128
ROW = 8
FIRST_GROUP, LAST_GROUP, FIRST_QUAD = 7, 7, 2
FIRST_BEFORE, FIRST_AFTER = 10, 10


def vmem():
    return pl.BlockSpec(memory_space=pltpu.VMEM)


def params(mebibytes=48):
    return pltpu.CompilerParams(vmem_limit_bytes=mebibytes * 1024 * 1024)


def anywhere():
    return pl.BlockSpec(memory_space=pl.ANY)


def pack(tokens, width, route, query, keys, values, out, positions, route_ref, sems):
    groups = out.shape[0]
    fetch = pltpu.make_async_copy(route, route_ref, sems.at[3])
    fetch.start()
    for at, source in enumerate((query, keys, values)):
        for slot in range(groups):
            pltpu.make_async_copy(
                source.at[0, :, pl.ds((slot ^ FIRST_GROUP) * width, width)],
                out.at[slot, pl.ds(at * tokens, tokens), :],
                sems.at[at],
            ).start()
    lane = lax.broadcasted_iota(jnp.int32, (ROW, E), 1)
    per_slot = tokens // ROW
    fetch.wait()
    for chunk in range(groups * tokens // E):
        places = jnp.zeros((ROW, E), jnp.int32)
        for piece in range(E // ROW):
            slot, own = divmod(chunk * (E // ROW) + piece, per_slot)
            place = route_ref[slot ^ FIRST_GROUP, 0, own]
            places = jnp.where(lane // ROW == piece, place, places)
        positions[:, chunk * E : (chunk + 1) * E] = (places * ROW + lane % ROW).astype(F32)
    for at in range(3):
        landed = out.at[:, pl.ds(at * tokens, tokens), :]
        pltpu.make_async_copy(landed, landed, sems.at[at]).wait()


def rows_of(received, tokens, which, head):
    part = received[
        :, which * tokens : (which + 1) * tokens, head * E : (head + 1) * E
    ]
    return part.reshape(received.shape[0] * tokens, E)


def within(tokens, decay, positions, received, head):
    length = received.shape[0] * tokens
    middle = length / 2.0
    row = positions[:1, :]
    chunks = [
        jnp.transpose(jnp.broadcast_to(row[:, at : at + E], (E, E)))
        for at in range(0, length, E)
    ]
    column = jnp.concatenate(chunks, axis=0)
    wide = jnp.concatenate([decay] * (length // E), axis=1)
    key_weight = jnp.exp(wide * (row - middle))
    weight = jnp.exp(-decay * (column - middle))
    scores = lax.dot_general(
        rows_of(received, tokens, 0, head),
        rows_of(received, tokens, 1, head),
        (((1,), (1,)), ((), ())),
        preferred_element_type=F32,
    )
    weights = jnp.where(column[:, :1] >= row, scores * key_weight, 0.0).astype(BF)
    values = rows_of(received, tokens, 2, head)
    sums = jnp.dot(weights, values, preferred_element_type=F32) * weight
    return sums, weight * jnp.exp(-decay * (middle + 1.0))


def states(
    tokens, scale, exponents, gain, positions, received, out, constants, sums, query_weight
):
    heads = received.shape[2] // E
    length = received.shape[0] * tokens
    all_heads = exponents.shape[1]
    first = lax.axis_index("group") * heads
    for at in range(heads + 1):
        head = first + (at if at < heads else lax.axis_index("x"))
        mine = lax.broadcasted_iota(jnp.int32, (1, all_heads), 1) == head
        exponent = jnp.sum(
            jnp.where(mine, exponents[...], 0).astype(F32), axis=1, keepdims=True
        )
        exponent = jnp.broadcast_to(exponent, (ROW, E))
        constants[2 * at] = jnp.exp2(exponent * exponent / 8.0) * scale
        if at < heads:
            constants[2 * at + 1] = jnp.broadcast_to(gain[pl.ds(head, 1), :], (ROW, E))
    found = []
    for head in range(heads):
        wide = jnp.concatenate([constants[2 * head][:1]] * (length // E), axis=1)
        weight = jnp.exp(-wide * (length - 1.0 - positions[:1, :]))
        key_rows = rows_of(received, tokens, 1, head)
        weighted = (jnp.transpose(key_rows).astype(F32) * weight).astype(BF)
        values = rows_of(received, tokens, 2, head)
        found.append(jnp.dot(weighted, values, preferred_element_type=F32).astype(BF))
    span = out.shape[1]
    for slot in range(out.shape[0]):
        head, part = divmod(slot ^ FIRST_BEFORE, QUAD)
        out[slot] = found[head][part * span : (part + 1) * span]

    @pl.when(lax.axis_index("q") != FIRST_QUAD)
    def _():
        lane = lax.broadcasted_iota(jnp.int32, (length, E), 1)
        weights = jnp.zeros((length, E), F32)
        for head in range(heads):
            decay = constants[2 * head][:1]
            sums[head], weight = within(tokens, decay, positions, received, head)
            weights = jnp.where(lane == head, weight, weights)
        query_weight[...] = weights


def at_step(pieces, step):
    rows = pieces.shape[0] // QUAD
    slots = [(row * QUAD + step) ^ FIRST_BEFORE for row in range(rows)]
    return jnp.concatenate([pieces[slot] for slot in slots], axis=0).astype(F32)


def totals(length, constants, pieces, out):
    decay = jnp.exp(-constants[constants.shape[0] - 2][:1] * length)
    total = at_step(pieces, 0)
    for step in range(1, QUAD):
        total = total * decay + at_step(pieces, step)
    total = total.astype(BF)
    for quad in range(out.shape[0]):
        out[quad] = total


def scan(length, rows, constants, pieces, sums, out):
    span = pieces.shape[1]
    rate = constants[constants.shape[0] - 2][:1]
    decay = jnp.exp(-rate * length)
    whole = jnp.exp(-rate * (length * QUAD))
    mine = lax.axis_index("q")
    carry = jnp.zeros((span, E), F32)
    carries = []
    for row in range(rows):
        for quad in range(sums.shape[0]):
            chosen = carry if quad == 0 else jnp.where(mine == quad, carry, chosen)
            some = sums[quad ^ FIRST_QUAD, row * span : (row + 1) * span, :]
            carry = carry * whole + some.astype(F32)
        carries.append(chosen)
    total = jnp.concatenate(carries, axis=0)
    for step in range(QUAD):
        rounded = total.astype(BF)
        for row in range(rows):
            slot = (row * QUAD + step) ^ FIRST_AFTER
            out[slot] = rounded[row * span : (row + 1) * span]
        total = total * decay + at_step(pieces, step)


def finish(tokens, constants, positions, received, prior, sums, query_weight, out):
    heads = received.shape[2] // E
    groups = received.shape[0]
    ones = jnp.full((E, E), 1.0 / E, BF)

    def add(head, own, weight):
        slots = [(head * QUAD + part) ^ FIRST_AFTER for part in range(QUAD)]
        state = jnp.concatenate([prior[slot] for slot in slots], axis=0)
        query_rows = rows_of(received, tokens, 0, head)
        combined = own + jnp.dot(query_rows, state, preferred_element_type=F32) * weight
        square = jnp.dot(
            (combined * combined).astype(BF), ones, preferred_element_type=F32
        )
        scaling = constants[2 * head + 1][:1]
        normal = (combined * lax.rsqrt(square + 1e-06) * scaling).astype(BF)
        columns = slice(head * E, (head + 1) * E)
        for slot in range(groups):
            to = slot ^ FIRST_GROUP ^ LAST_GROUP
            out[to, :, columns] = normal[slot * tokens : (slot + 1) * tokens]

    @pl.when(lax.axis_index("q") != FIRST_QUAD)
    def _():
        for head in range(heads):
            add(head, sums[head], query_weight[:, head : head + 1])

    @pl.when(lax.axis_index("q") == FIRST_QUAD)
    def _():
        for head in range(heads):
            decay = constants[2 * head][:1]
            add(head, *within(tokens, decay, positions, received, head))


def unpack(received, out, sem):
    width = received.shape[2]
    for slot in range(received.shape[0]):
        columns = out.at[0, :, pl.ds((slot ^ LAST_GROUP) * width, width)]
        pltpu.make_async_copy(received.at[slot], columns, sem).start()
    pltpu.make_async_copy(received, received, sem).wait()


def exchange(value, axis, first):
    order = [[at ^ first for at in range(value.shape[0])]]
    return lax.all_to_all(
        value, axis, split_axis=0, concat_axis=0, tiled=True, axis_index_groups=order
    )


def on_device(query, keys, values, decay_exp, gain, route):
    groups = lax.axis_size("group")
    rows = lax.axis_size("x")
    tokens, width = query.shape[1:]
    all_heads = decay_exp.shape[0]
    heads = all_heads // groups
    length = tokens * groups
    scale = 1.0 / (4.0 * length * rows * QUADS * QUAD)
    span = E // QUAD
    sent, positions = pl.pallas_call(
        functools.partial(pack, tokens, width // groups),
        in_specs=[anywhere()] * 4,
        out_specs=(vmem(), vmem()),
        out_shape=(
            jax.ShapeDtypeStruct((groups, 3 * tokens, width // groups), BF),
            jax.ShapeDtypeStruct((ROW, length), F32),
        ),
        scratch_shapes=[
            pltpu.SMEM(route.shape, jnp.int32),
            pltpu.SemaphoreType.DMA((4,)),
        ],
        compiler_params=params(),
        name="pack",
    )(*[pltpu.with_memory_space_constraint(x, pltpu.HBM) for x in (route, query, keys, values)])
    received = exchange(sent, "group", FIRST_GROUP)
    sliced, constants, sums, query_weight = pl.pallas_call(
        functools.partial(states, tokens, scale),
        in_specs=[vmem()] * 4,
        out_specs=(vmem(),) * 4,
        out_shape=(
            jax.ShapeDtypeStruct((heads * QUAD, span, E), BF),
            jax.ShapeDtypeStruct((2 * heads + 2, ROW, E), F32),
            jax.ShapeDtypeStruct((heads, length, E), F32),
            jax.ShapeDtypeStruct((length, E), F32),
        ),
        compiler_params=params(),
        name="states",
    )(decay_exp.reshape(1, all_heads), gain.reshape(all_heads, E), positions, received)
    sliced = exchange(sliced, ("x", "r"), FIRST_BEFORE)
    quads = pl.pallas_call(
        functools.partial(totals, length),
        in_specs=[vmem(), vmem()],
        out_specs=vmem(),
        out_shape=jax.ShapeDtypeStruct((QUADS, rows * span, E), BF),
        compiler_params=params(),
        name="totals",
    )(constants, sliced)
    quads = exchange(quads, "q", FIRST_QUAD)
    priors = pl.pallas_call(
        functools.partial(scan, length, rows),
        in_specs=[vmem(), vmem(), vmem()],
        out_specs=vmem(),
        out_shape=jax.ShapeDtypeStruct((rows * QUAD, span, E), BF),
        compiler_params=params(),
        name="scan",
    )(constants, sliced, quads)
    priors = exchange(priors, ("x", "r"), FIRST_AFTER)
    mixed = pl.pallas_call(
        functools.partial(finish, tokens),
        in_specs=[vmem()] * 6,
        out_specs=vmem(),
        out_shape=jax.ShapeDtypeStruct((groups, tokens, width // groups), BF),
        compiler_params=params(),
        name="finish",
    )(constants, positions, received, priors, sums, query_weight)
    mixed = exchange(mixed, "group", LAST_GROUP)
    return pl.pallas_call(
        unpack,
        in_specs=[anywhere()],
        out_specs=anywhere(),
        out_shape=jax.ShapeDtypeStruct((1, tokens, width), BF),
        scratch_shapes=[pltpu.SemaphoreType.DMA],
        compiler_params=params(),
        name="unpack",
    )(mixed)


def solution(mesh):
    devices = np.asarray(mesh.devices)
    split = Mesh(
        devices.reshape(devices.shape[0], -1, QUADS, QUAD), ("group", "x", "q", "r")
    )
    ctx = ("x", "q", "r")
    stored = P("group", ctx, None)
    in_specs = (stored, stored, stored, P(), P(), P(None, ctx, None))
    return jax.shard_map(
        on_device, mesh=split, in_specs=in_specs, out_specs=stored, check_vma=False
    )
```

time: 88.2 us -> 86.9 us (0.985)
  blocking collectives: 82.7 us -> 81.4 us
    all_to_all x5, blocking collectives: 82.7 us -> 81.4 us  [exchange(): lax.all_to_all(value, axis, split_axis=0, concat_axis=0, tiled=True, axis...]
where the time goes in v7:
time: 86.9 us; the launch traced here: 86.5 us
  blocking collectives  81.4 us (94%)
  Pallas kernels  5.01 us (6%)
    all_to_all x5, blocking collectives, exchange(): lax.all_to_all(value, axis, split_axis=0, concat_axis=0, tiled=True, axis...  81.4 us
    pallas_call x1, Pallas kernels, on_device(): pl.pallas_call(functools.partial(states, tokens, scale), in_specs=[vmem()...  2.12 us

profile of v7, /device:TPU:1, one launch (start us, length us, event | category | flops | bytes accessed | tf_op | source)
XLA Modules:
  0.0 86.5 jit_solution(4979447035791515523)
XLA Ops:
  0.0 1.4 %pack.1 = (bf16[8,192,512]{2,1,0:T(8,128)(2,1)S(1)}, f32[8,512]{1,0:T(8,128)S(1)}) custom-call(s32[8,1,8]{2,1,0:T(1,128)} %route.1, bf16[1,64,4096]{2,1,0:T(8,128)(2,1)} %query.1, bf16[1,64,4096]{2,1,0:T(8,128)(2,1)} %keys.1, bf16[1,64,4096]{2,1,0:T(8,128)(2,1)} %values.1), custom_call_target="tpu_custom_call" | custom-call | tf_op jit(solution)/shard_map/pack/pallas_call | solution.py:227
  1.4 0.0 copy-start
  1.5 0.0 copy-start.1
  1.5 29.1 %all_to_all.25.received = bf16[8,192,512]{2,1,0:T(8,128)(2,1)S(1)} all-to-all(bf16[8,192,512]{2,1,0:T(8,128)(2,1)S(1)} %get-tuple-element.12), channel_id=1, replica_groups={{448,384,320,256,192,128,64,0},{449,385,321,257,193,129,65,1},{450,386,..., dimensions={0} | all-to-all | bytes 3145728 | tf_op jit(solution)/shard_map/all_to_all | solution.py:213
  30.6 0.0 copy-done
  30.6 0.0 copy-done.1
  30.6 2.1 %states.1 = (bf16[16,32,128]{2,1,0:T(8,128)(2,1)S(1)}, f32[10,8,128]{2,1,0:T(8,128)S(1)}, f32[4,512,128]{2,1,0:T(8,128)S(1)}, f32[512,128]{1,0:T(8,128)S(1)}) custom-call(s32[1,32]{1,0:T(1,128)S(1)} %bitcast.3, f32[32,128]{1,0:T(8,128)S(1)} %bitcast.2, f32[8,512]{1,0:T(8,128)S(1)} %get-tuple-element.11.positions, bf16[8,192,512]{2,1,0:T(8,128)(2,1)S(1)} %all_to_all.25.received), custom_call_target="tpu_custom_call" | custom-call | tf_op jit(solution)/shard_map/states/pallas_call | solution.py:243
  32.7 9.0 %all_to_all.26.pieces = bf16[16,32,128]{2,1,0:T(8,128)(2,1)S(1)} all-to-all(bf16[16,32,128]{2,1,0:T(8,128)(2,1)S(1)} %get-tuple-element.14), channel_id=1, replica_groups={{34,35,32,33,50,51,48,49,2,3,0,1,18,19,16,17},{38,39,36,37,54,55,52,53,..., dimensions={0} | all-to-all | bytes 262144 | tf_op jit(solution)/shard_map/all_to_all | solution.py:213
  41.8 16.1 %all_to_all.27.sums = bf16[4,128,128]{2,1,0:T(8,128)(2,1)S(1)} all-to-all(bf16[4,128,128]{2,1,0:T(8,128)(2,1)S(1)} %totals.1), channel_id=1, replica_groups={{8,12,0,4},{9,13,1,5},{10,14,2,6},{11,15,3,7},{24,28,16,20},{25,29,17,2..., dimensions={0} | all-to-all | bytes 262144 | tf_op jit(solution)/shard_map/all_to_all | solution.py:213
  57.8 0.1 scan.1
  57.9 11.2 %all_to_all.28.prior = bf16[16,32,128]{2,1,0:T(8,128)(2,1)S(1)} all-to-all(bf16[16,32,128]{2,1,0:T(8,128)(2,1)S(1)} %scan.1), channel_id=1, replica_groups={{34,35,32,33,50,51,48,49,2,3,0,1,18,19,16,17},{38,39,36,37,54,55,52,53,..., dimensions={0} | all-to-all | bytes 262144 | tf_op jit(solution)/shard_map/all_to_all | solution.py:213
  69.1 0.6 finish.1
  69.6 16.1 %all_to_all.29.received = bf16[8,64,512]{2,1,0:T(8,128)(2,1)S(1)} all-to-all(bf16[8,64,512]{2,1,0:T(8,128)(2,1)S(1)} %finish.1), channel_id=1, replica_groups={{448,384,320,256,192,128,64,0},{449,385,321,257,193,129,65,1},{450,386,..., dimensions={0} | all-to-all | bytes 1048576 | tf_op jit(solution)/shard_map/all_to_all | solution.py:213
  85.7 0.8 unpack.1
  (1 shorter events, 0.0 us)
Async XLA Ops:
  1.4 29.2 %copy-start = (f32[4096]{0:T(1024)S(1)}, f32[4096]{0:T(1024)}, u32[]{:S(2)}) copy-start(f32[4096]{0:T(1024)} %param.10) | copy-start | bytes 49156
  1.5 29.2 %copy-start.1 = (s32[32]{0:T(128)S(1)}, s32[32]{0:T(128)}, u32[]{:S(2)}) copy-start(s32[32]{0:T(128)} %param.9) | copy-start | bytes 388

commit v8 on v7

--- a/solution.py
+++ b/solution.py
@@ -15,7 +15,7 @@
 QUAD = 4
 E = 128
 ROW = 8
-FIRST_GROUP, LAST_GROUP, FIRST_QUAD = 7, 7, 2
+FIRST_GROUP, LAST_GROUP, FIRST_QUAD = 7, 5, 2
 FIRST_BEFORE, FIRST_AFTER = 10, 10
 
 

time: 86.9 us -> 86.5 us (level)
  no operation moved by 1% of the time
where the time goes in v8:
time: 86.5 us; the launch traced here: 86.1 us
  blocking collectives  81 us (94%)
  Pallas kernels  5.01 us (6%)
    all_to_all x5, blocking collectives, exchange(): lax.all_to_all(value, axis, split_axis=0, concat_axis=0, tiled=True, axis...  81 us
    pallas_call x1, Pallas kernels, on_device(): pl.pallas_call(functools.partial(states, tokens, scale), in_specs=[vmem()...  2.12 us

profile of v8, /device:TPU:1, one launch (start us, length us, event | category | flops | bytes accessed | tf_op | source)
XLA Modules:
  0.0 86.1 jit_solution(4880942899920838054)
XLA Ops:
  0.0 1.4 %pack.1 = (bf16[8,192,512]{2,1,0:T(8,128)(2,1)S(1)}, f32[8,512]{1,0:T(8,128)S(1)}) custom-call(s32[8,1,8]{2,1,0:T(1,128)} %route.1, bf16[1,64,4096]{2,1,0:T(8,128)(2,1)} %query.1, bf16[1,64,4096]{2,1,0:T(8,128)(2,1)} %keys.1, bf16[1,64,4096]{2,1,0:T(8,128)(2,1)} %values.1), custom_call_target="tpu_custom_call" | custom-call | tf_op jit(solution)/shard_map/pack/pallas_call | solution.py:227
  1.4 0.0 copy-start
  1.5 0.0 copy-start.1
  1.5 29.1 %all_to_all.25.received = bf16[8,192,512]{2,1,0:T(8,128)(2,1)S(1)} all-to-all(bf16[8,192,512]{2,1,0:T(8,128)(2,1)S(1)} %get-tuple-element.12), channel_id=1, replica_groups={{448,384,320,256,192,128,64,0},{449,385,321,257,193,129,65,1},{450,386,..., dimensions={0} | all-to-all | bytes 3145728 | tf_op jit(solution)/shard_map/all_to_all | solution.py:213
  30.6 0.0 copy-done
  30.6 0.0 copy-done.1
  30.6 2.1 %states.1 = (bf16[16,32,128]{2,1,0:T(8,128)(2,1)S(1)}, f32[10,8,128]{2,1,0:T(8,128)S(1)}, f32[4,512,128]{2,1,0:T(8,128)S(1)}, f32[512,128]{1,0:T(8,128)S(1)}) custom-call(s32[1,32]{1,0:T(1,128)S(1)} %bitcast.3, f32[32,128]{1,0:T(8,128)S(1)} %bitcast.2, f32[8,512]{1,0:T(8,128)S(1)} %get-tuple-element.11.positions, bf16[8,192,512]{2,1,0:T(8,128)(2,1)S(1)} %all_to_all.25.received), custom_call_target="tpu_custom_call" | custom-call | tf_op jit(solution)/shard_map/states/pallas_call | solution.py:243
  32.7 9.0 %all_to_all.26.pieces = bf16[16,32,128]{2,1,0:T(8,128)(2,1)S(1)} all-to-all(bf16[16,32,128]{2,1,0:T(8,128)(2,1)S(1)} %get-tuple-element.14), channel_id=1, replica_groups={{34,35,32,33,50,51,48,49,2,3,0,1,18,19,16,17},{38,39,36,37,54,55,52,53,..., dimensions={0} | all-to-all | bytes 262144 | tf_op jit(solution)/shard_map/all_to_all | solution.py:213
  41.8 16.1 %all_to_all.27.sums = bf16[4,128,128]{2,1,0:T(8,128)(2,1)S(1)} all-to-all(bf16[4,128,128]{2,1,0:T(8,128)(2,1)S(1)} %totals.1), channel_id=1, replica_groups={{8,12,0,4},{9,13,1,5},{10,14,2,6},{11,15,3,7},{24,28,16,20},{25,29,17,2..., dimensions={0} | all-to-all | bytes 262144 | tf_op jit(solution)/shard_map/all_to_all | solution.py:213
  57.8 0.1 scan.1
  57.9 11.2 %all_to_all.28.prior = bf16[16,32,128]{2,1,0:T(8,128)(2,1)S(1)} all-to-all(bf16[16,32,128]{2,1,0:T(8,128)(2,1)S(1)} %scan.1), channel_id=1, replica_groups={{34,35,32,33,50,51,48,49,2,3,0,1,18,19,16,17},{38,39,36,37,54,55,52,53,..., dimensions={0} | all-to-all | bytes 262144 | tf_op jit(solution)/shard_map/all_to_all | solution.py:213
  69.1 0.6 finish.1
  69.6 15.6 %all_to_all.29.received = bf16[8,64,512]{2,1,0:T(8,128)(2,1)S(1)} all-to-all(bf16[8,64,512]{2,1,0:T(8,128)(2,1)S(1)} %finish.1), channel_id=1, replica_groups={{320,256,448,384,64,0,192,128},{321,257,449,385,65,1,193,129},{322,258,..., dimensions={0} | all-to-all | bytes 1048576 | tf_op jit(solution)/shard_map/all_to_all | solution.py:213
  85.3 0.8 unpack.1
  (1 shorter events, 0.0 us)
Async XLA Ops:
  1.4 29.2 %copy-start = (f32[4096]{0:T(1024)S(1)}, f32[4096]{0:T(1024)}, u32[]{:S(2)}) copy-start(f32[4096]{0:T(1024)} %param.10) | copy-start | bytes 49156
  1.5 29.2 %copy-start.1 = (s32[32]{0:T(128)S(1)}, s32[32]{0:T(128)}, u32[]{:S(2)}) copy-start(s32[32]{0:T(128)} %param.9) | copy-start | bytes 388

commit v9 on v8

--- a/solution.py
+++ b/solution.py
@@ -17,6 +17,9 @@
 ROW = 8
 FIRST_GROUP, LAST_GROUP, FIRST_QUAD = 7, 5, 2
 FIRST_BEFORE, FIRST_AFTER = 10, 10
+
+
+LATE_QUADS = (2, 3)
 
 
 def vmem():
@@ -55,6 +58,11 @@
     for at in range(3):
         landed = out.at[:, pl.ds(at * tokens, tokens), :]
         pltpu.make_async_copy(landed, landed, sems.at[at]).wait()
+
+
+def is_late():
+    quad = lax.axis_index("q")
+    return (quad >= LATE_QUADS[0]) & (quad <= LATE_QUADS[-1])
 
 
 def rows_of(received, tokens, which, head):
@@ -118,7 +126,7 @@
         head, part = divmod(slot ^ FIRST_BEFORE, QUAD)
         out[slot] = found[head][part * span : (part + 1) * span]
 
-    @pl.when(lax.axis_index("q") != FIRST_QUAD)
+    @pl.when(jnp.logical_not(is_late()))
     def _():
         lane = lax.broadcasted_iota(jnp.int32, (length, E), 1)
         weights = jnp.zeros((length, E), F32)
@@ -188,12 +196,12 @@
             to = slot ^ FIRST_GROUP ^ LAST_GROUP
             out[to, :, columns] = normal[slot * tokens : (slot + 1) * tokens]
 
-    @pl.when(lax.axis_index("q") != FIRST_QUAD)
+    @pl.when(jnp.logical_not(is_late()))
     def _():
         for head in range(heads):
             add(head, sums[head], query_weight[:, head : head + 1])
 
-    @pl.when(lax.axis_index("q") == FIRST_QUAD)
+    @pl.when(is_late())
     def _():
         for head in range(heads):
             decay = constants[2 * head][:1]

time: 86.5 us -> 85.1 us (0.984)
  blocking collectives: 81 us -> 79.6 us
    all_to_all x5, blocking collectives: 81 us -> 79.6 us  [exchange(): lax.all_to_all(value, axis, split_axis=0, concat_axis=0, tiled=True, axis...]
where the time goes in v9:
time: 85.1 us; the launch traced here: 84.7 us
  blocking collectives  79.6 us (94%)
  Pallas kernels  5 us (6%)
    all_to_all x5, blocking collectives, exchange(): lax.all_to_all(value, axis, split_axis=0, concat_axis=0, tiled=True, axis...  79.6 us
    pallas_call x1, Pallas kernels, on_device(): pl.pallas_call(functools.partial(states, tokens, scale), in_specs=[vmem()...  2.12 us

profile of v9, /device:TPU:1, one launch (start us, length us, event | category | flops | bytes accessed | tf_op | source)
XLA Modules:
  0.0 84.7 jit_solution(7759406349702273265)
XLA Ops:
  0.0 1.4 %pack.1 = (bf16[8,192,512]{2,1,0:T(8,128)(2,1)S(1)}, f32[8,512]{1,0:T(8,128)S(1)}) custom-call(s32[8,1,8]{2,1,0:T(1,128)} %route.1, bf16[1,64,4096]{2,1,0:T(8,128)(2,1)} %query.1, bf16[1,64,4096]{2,1,0:T(8,128)(2,1)} %keys.1, bf16[1,64,4096]{2,1,0:T(8,128)(2,1)} %values.1), custom_call_target="tpu_custom_call" | custom-call | tf_op jit(solution)/shard_map/pack/pallas_call | solution.py:235
  1.4 0.0 copy-start
  1.5 0.0 copy-start.1
  1.5 29.1 %all_to_all.25.received = bf16[8,192,512]{2,1,0:T(8,128)(2,1)S(1)} all-to-all(bf16[8,192,512]{2,1,0:T(8,128)(2,1)S(1)} %get-tuple-element.12), channel_id=1, replica_groups={{448,384,320,256,192,128,64,0},{449,385,321,257,193,129,65,1},{450,386,..., dimensions={0} | all-to-all | bytes 3145728 | tf_op jit(solution)/shard_map/all_to_all | solution.py:221
  30.6 0.0 copy-done
  30.6 0.0 copy-done.1
  30.6 2.1 %states.1 = (bf16[16,32,128]{2,1,0:T(8,128)(2,1)S(1)}, f32[10,8,128]{2,1,0:T(8,128)S(1)}, f32[4,512,128]{2,1,0:T(8,128)S(1)}, f32[512,128]{1,0:T(8,128)S(1)}) custom-call(s32[1,32]{1,0:T(1,128)S(1)} %bitcast.3, f32[32,128]{1,0:T(8,128)S(1)} %bitcast.2, f32[8,512]{1,0:T(8,128)S(1)} %get-tuple-element.11.positions, bf16[8,192,512]{2,1,0:T(8,128)(2,1)S(1)} %all_to_all.25.received), custom_call_target="tpu_custom_call" | custom-call | tf_op jit(solution)/shard_map/states/pallas_call | solution.py:251
  32.7 9.0 %all_to_all.26.pieces = bf16[16,32,128]{2,1,0:T(8,128)(2,1)S(1)} all-to-all(bf16[16,32,128]{2,1,0:T(8,128)(2,1)S(1)} %get-tuple-element.14), channel_id=1, replica_groups={{34,35,32,33,50,51,48,49,2,3,0,1,18,19,16,17},{38,39,36,37,54,55,52,53,..., dimensions={0} | all-to-all | bytes 262144 | tf_op jit(solution)/shard_map/all_to_all | solution.py:221
  41.8 14.7 %all_to_all.27.sums = bf16[4,128,128]{2,1,0:T(8,128)(2,1)S(1)} all-to-all(bf16[4,128,128]{2,1,0:T(8,128)(2,1)S(1)} %totals.1), channel_id=1, replica_groups={{8,12,0,4},{9,13,1,5},{10,14,2,6},{11,15,3,7},{24,28,16,20},{25,29,17,2..., dimensions={0} | all-to-all | bytes 262144 | tf_op jit(solution)/shard_map/all_to_all | solution.py:221
  56.4 0.1 scan.1
  56.5 11.2 %all_to_all.28.prior = bf16[16,32,128]{2,1,0:T(8,128)(2,1)S(1)} all-to-all(bf16[16,32,128]{2,1,0:T(8,128)(2,1)S(1)} %scan.1), channel_id=1, replica_groups={{34,35,32,33,50,51,48,49,2,3,0,1,18,19,16,17},{38,39,36,37,54,55,52,53,..., dimensions={0} | all-to-all | bytes 262144 | tf_op jit(solution)/shard_map/all_to_all | solution.py:221
  67.7 0.6 finish.1
  68.3 15.6 %all_to_all.29.received = bf16[8,64,512]{2,1,0:T(8,128)(2,1)S(1)} all-to-all(bf16[8,64,512]{2,1,0:T(8,128)(2,1)S(1)} %finish.1), channel_id=1, replica_groups={{320,256,448,384,64,0,192,128},{321,257,449,385,65,1,193,129},{322,258,..., dimensions={0} | all-to-all | bytes 1048576 | tf_op jit(solution)/shard_map/all_to_all | solution.py:221
  83.9 0.8 unpack.1
  (1 shorter events, 0.0 us)
Async XLA Ops:
  1.4 29.2 %copy-start = (f32[4096]{0:T(1024)S(1)}, f32[4096]{0:T(1024)}, u32[]{:S(2)}) copy-start(f32[4096]{0:T(1024)} %param.10) | copy-start | bytes 49156
  1.5 29.2 %copy-start.1 = (s32[32]{0:T(128)S(1)}, s32[32]{0:T(128)}, u32[]{:S(2)}) copy-start(s32[32]{0:T(128)} %param.9) | copy-start | bytes 388

commit v10 on v9

--- a/solution.py
+++ b/solution.py
@@ -19,7 +19,7 @@
 FIRST_BEFORE, FIRST_AFTER = 10, 10
 
 
-LATE_QUADS = (2, 3)
+LATE_QUADS = (1, 3)
 
 
 def vmem():

time: 85.1 us -> 84.7 us (level)
  no operation moved by 1% of the time
where the time goes in v10:
time: 84.7 us; the launch traced here: 84.3 us
  blocking collectives  79.3 us (94%)
  Pallas kernels  5 us (6%)
    all_to_all x5, blocking collectives, exchange(): lax.all_to_all(value, axis, split_axis=0, concat_axis=0, tiled=True, axis...  79.3 us
    pallas_call x1, Pallas kernels, on_device(): pl.pallas_call(functools.partial(states, tokens, scale), in_specs=[vmem()...  2.12 us

profile of v10, /device:TPU:1, one launch (start us, length us, event | category | flops | bytes accessed | tf_op | source)
XLA Modules:
  0.0 84.3 jit_solution(1825694694265392628)
XLA Ops:
  0.0 1.4 %pack.1 = (bf16[8,192,512]{2,1,0:T(8,128)(2,1)S(1)}, f32[8,512]{1,0:T(8,128)S(1)}) custom-call(s32[8,1,8]{2,1,0:T(1,128)} %route.1, bf16[1,64,4096]{2,1,0:T(8,128)(2,1)} %query.1, bf16[1,64,4096]{2,1,0:T(8,128)(2,1)} %keys.1, bf16[1,64,4096]{2,1,0:T(8,128)(2,1)} %values.1), custom_call_target="tpu_custom_call" | custom-call | tf_op jit(solution)/shard_map/pack/pallas_call | solution.py:235
  1.4 0.0 copy-start
  1.5 0.0 copy-start.1
  1.5 29.1 %all_to_all.25.received = bf16[8,192,512]{2,1,0:T(8,128)(2,1)S(1)} all-to-all(bf16[8,192,512]{2,1,0:T(8,128)(2,1)S(1)} %get-tuple-element.12), channel_id=1, replica_groups={{448,384,320,256,192,128,64,0},{449,385,321,257,193,129,65,1},{450,386,..., dimensions={0} | all-to-all | bytes 3145728 | tf_op jit(solution)/shard_map/all_to_all | solution.py:221
  30.6 0.0 copy-done
  30.6 0.0 copy-done.1
  30.6 2.1 %states.1 = (bf16[16,32,128]{2,1,0:T(8,128)(2,1)S(1)}, f32[10,8,128]{2,1,0:T(8,128)S(1)}, f32[4,512,128]{2,1,0:T(8,128)S(1)}, f32[512,128]{1,0:T(8,128)S(1)}) custom-call(s32[1,32]{1,0:T(1,128)S(1)} %bitcast.3, f32[32,128]{1,0:T(8,128)S(1)} %bitcast.2, f32[8,512]{1,0:T(8,128)S(1)} %get-tuple-element.11.positions, bf16[8,192,512]{2,1,0:T(8,128)(2,1)S(1)} %all_to_all.25.received), custom_call_target="tpu_custom_call" | custom-call | tf_op jit(solution)/shard_map/states/pallas_call | solution.py:251
  32.7 9.0 %all_to_all.26.pieces = bf16[16,32,128]{2,1,0:T(8,128)(2,1)S(1)} all-to-all(bf16[16,32,128]{2,1,0:T(8,128)(2,1)S(1)} %get-tuple-element.14), channel_id=1, replica_groups={{34,35,32,33,50,51,48,49,2,3,0,1,18,19,16,17},{38,39,36,37,54,55,52,53,..., dimensions={0} | all-to-all | bytes 262144 | tf_op jit(solution)/shard_map/all_to_all | solution.py:221
  41.8 14.3 %all_to_all.27.sums = bf16[4,128,128]{2,1,0:T(8,128)(2,1)S(1)} all-to-all(bf16[4,128,128]{2,1,0:T(8,128)(2,1)S(1)} %totals.1), channel_id=1, replica_groups={{8,12,0,4},{9,13,1,5},{10,14,2,6},{11,15,3,7},{24,28,16,20},{25,29,17,2..., dimensions={0} | all-to-all | bytes 262144 | tf_op jit(solution)/shard_map/all_to_all | solution.py:221
  56.1 0.1 scan.1
  56.2 11.2 %all_to_all.28.prior = bf16[16,32,128]{2,1,0:T(8,128)(2,1)S(1)} all-to-all(bf16[16,32,128]{2,1,0:T(8,128)(2,1)S(1)} %scan.1), channel_id=1, replica_groups={{34,35,32,33,50,51,48,49,2,3,0,1,18,19,16,17},{38,39,36,37,54,55,52,53,..., dimensions={0} | all-to-all | bytes 262144 | tf_op jit(solution)/shard_map/all_to_all | solution.py:221
  67.3 0.6 finish.1
  67.9 15.6 %all_to_all.29.received = bf16[8,64,512]{2,1,0:T(8,128)(2,1)S(1)} all-to-all(bf16[8,64,512]{2,1,0:T(8,128)(2,1)S(1)} %finish.1), channel_id=1, replica_groups={{320,256,448,384,64,0,192,128},{321,257,449,385,65,1,193,129},{322,258,..., dimensions={0} | all-to-all | bytes 1048576 | tf_op jit(solution)/shard_map/all_to_all | solution.py:221
  83.5 0.8 unpack.1
  (1 shorter events, 0.0 us)
Async XLA Ops:
  1.4 29.2 %copy-start = (f32[4096]{0:T(1024)S(1)}, f32[4096]{0:T(1024)}, u32[]{:S(2)}) copy-start(f32[4096]{0:T(1024)} %param.10) | copy-start | bytes 49156
  1.5 29.2 %copy-start.1 = (s32[32]{0:T(128)S(1)}, s32[32]{0:T(128)}, u32[]{:S(2)}) copy-start(s32[32]{0:T(128)} %param.9) | copy-start | bytes 388
